TPU v7x, 32 devices: a whole 2x2x4 slice. The times are simulated.
32 devices in a mesh: group: 2 (over y), shot: 4 (over z), line: 2 (over x), tm: 2 (over core).
Axes of the slice: x: 2, y: 2, z: 4, core: 2. Of those that a mesh axis runs over, the one named last changes fastest.
Arguments:
- initial_guess: bfloat16 [8, 256, 1024], P(('group', 'shot'), 'line', 'tm'), parts along dimension 0
- measured_mixtures: bfloat16 [4, 256, 1024], P('group', 'line'), parts along dimension 0
- launch_lags: int32 [8], P('group'), parts along dimension 0, may hold values from 0 to 127, as said below
- source_launch_order: int32 [8], P('group'), parts along dimension 0, may hold values from 0 to 3, each once
- station_portion_tallies: int32 [16], P('group'), parts along dimension 0, may hold values from 1 to 32, 128 in all
- source_entry_kernel: bfloat16 [4, 3, 64], replicated, may hold values from -1.75 to 1.75
- source_spaced_kernel: bfloat16 [3, 64, 64], replicated, may hold values from -0.4375 to 0.4375
- source_exit_kernel: bfloat16 [4, 64], replicated, may hold values from -0.5 to 0.5
- source_inner_offsets: float32 [2, 64], replicated, may hold values from -3 to 3
- station_entry_kernel: bfloat16 [4, 3, 64], replicated, may hold values from -1.75 to 1.75
- station_spaced_kernel: bfloat16 [3, 64, 64], replicated, may hold values from -0.4375 to 0.4375
- station_exit_kernel: bfloat16 [4, 64], replicated, may hold values from -0.5 to 0.5
- station_inner_offsets: float32 [2, 64], replicated, may hold values from -3 to 3
- learned_pace_factors: float32 [2], replicated, may hold values from 0.3 to 0.8
Outputs:
- deblended: bfloat16 [8, 256, 1024], P(('group', 'shot'), 'line', 'tm'), parts along dimension 0
There are 2 independent parts, one for each index of `group`. A program takes and returns all parts, laid end to end along the dimension named above; an argument that names none is the same for every part. Nothing has to cross between parts.
Inputs may be any that keep to these rules, and one draw needn't show every extreme that they name: `launch_lags`: 0 and 127 both occur. `source_launch_order`: each shot once. `station_portion_tallies`: the counts sum to 128 and the largest equals 32.
All inputs are finite; a program needn't handle non-finite values.
Results may differ from a plain program's by a relative error of at most 0.013.
Values may be sent and summed in bfloat16 or wider, within the bound.
No kernel may reach another device: no remote copies, remote signals or barrier semaphores. Data moves between devices by JAX's collectives and lax.ppermute only.
A program may use at most 64 MiB of HBM per device.

v0:
```python
import functools

import jax
import jax.numpy as jnp
from jax import lax
from jax.experimental import pallas as pl
from jax.experimental.pallas import tpu as pltpu
from jax.sharding import PartitionSpec as P

RPL = 16
DMAX = 128
ITERS = 2
EPSILON = 1e-05

SLAB = 128
HALF = 64
FEAT = 64
GROUP = 4
WIDE = GROUP * FEAT
QS = SLAB // (2 * GROUP)
QH = QS // 2
assert QH == 8
ONES = 3 * HALF + 6
VMEM_LIMIT = 24 * 1024 * 1024
VMEM_FULL = 63 * 1024 * 1024

BF = jnp.bfloat16
F32 = jnp.float32


def split_bias(bias):
    high = bias.astype(BF).astype(F32)
    middle = (bias - high).astype(BF).astype(F32)
    return high, middle, bias - high - middle


def iota(shape, axis):
    return lax.broadcasted_iota(jnp.int32, shape, axis)


def picks(mask):
    return mask.astype(F32).astype(BF)


def start_of(q):
    return 16 * (q // 2) + 2 * (q % 2)


def prepare_kernel(bundle, bias, o_in, o_out, rhs, cols):
    rhs[...] = jnp.zeros_like(rhs)
    cols[...] = jnp.zeros_like(cols)
    parts = split_bias(bias[0:1, :])
    exits = bundle[3 * FEAT : 3 * FEAT + 16, :].astype(F32)[0:4]
    for p in range(GROUP):
        lanes = slice(p * FEAT, (p + 1) * FEAT)
        for c in range(3):
            row = 3 * FEAT + 16 * (c + 1)
            rhs[p * 32 + c * 8 : p * 32 + c * 8 + 4, lanes] = bundle[row : row + 16, :].astype(F32)[0:4]
            rhs[p * 32 + 24 + c : p * 32 + 25 + c, lanes] = parts[c]
        cols[p * 8 : p * 8 + 4, lanes] = exits
    taps = rhs[...].astype(BF)
    row, col = iota((WIDE, SLAB), 0), iota((WIDE, SLAB), 1)
    channel, j, target = (col >> 3) & 3, col & 7, 4 * (col >> 5) + (col & 7) - 1
    rest = row - 3 * HALF
    sample = jnp.where(rest < 0, row & (HALF - 1), jnp.where(rest & 1 == 1, HALF, -1))
    same = (jnp.where(rest < 0, row >> 6, rest >> 1) == channel) & (channel < 3) & (j < 4)
    offset = jnp.where(same, sample - target, -SLAB)
    ones = (channel == 3) & (j < 3) & (row == ONES + j)
    for q in range(QH):
        chosen = picks((offset == start_of(q)) | ones)
        o_in[q] = jnp.dot(chosen, taps, preferred_element_type=F32).astype(BF)
    o_in[QH:] = jnp.zeros((2, WIDE, WIDE), BF)
    for a, at in [(0, 0), (1, 1), (2, 2), (3, 3), (4, 4), (-1, 5)]:
        for b in range(GROUP):
            if abs(a - b) <= 1:
                tap = a - b + 1
                rows, lanes = slice(at % 4 * FEAT, (at % 4 + 1) * FEAT), slice(b * FEAT, (b + 1) * FEAT)
                o_in[QH + at // 4, rows, lanes] = bundle[tap * FEAT : (tap + 1) * FEAT, :]
    row = iota((16, FEAT), 0)
    below = jnp.zeros((16, FEAT), F32)
    for i, part in enumerate(split_bias(bias[1:2, :])):
        below = jnp.where(row == i, part, below)
    for b in range(GROUP):
        o_in[QH + 1, SLAB : SLAB + 16, b * FEAT : (b + 1) * FEAT] = below.astype(BF)
    row, col = iota((SLAB, SLAB), 0), iota((SLAB, SLAB), 1)
    p, j = row >> 3, row & 7
    offset = jnp.where((p < GROUP) & (j < 4), col - (4 * p + j - 1), -SLAB)
    back = jnp.transpose(cols[...]).astype(BF)
    follows = (p == GROUP - 1) & (j == 3) & (col == 0)
    precedes = (row == 0) & (col == SLAB - 1)
    for q in range(QS + 2):
        chosen = picks(offset == start_of(q) if q < QS else [follows, precedes][q - QS])
        o_out[q] = jnp.dot(back, chosen, preferred_element_type=F32).astype(BF)


def pack_kernel(plan, traces, *refs):
    outs, held, done = refs[:4], refs[4], refs[5]
    _, _, at_tm, _, at_line = places(plan, True)
    block = traces.shape[0]
    copy = pltpu.make_async_copy(traces, held, done)
    copy.start()
    lines = plan.lines
    half = block // 2
    row, col = iota((block, block), 0), iota((block, block), 1)
    spot, line = split_index(row, lines)
    d, spot = split_index(spot, half // lines)
    order = picks(col == line * RPL + (at_tm ^ d) * (half // lines) + spot)
    row, col = iota((32, block), 0), iota((32, block), 1)
    d, spot = split_index(row, 16)
    sent = jnp.where(at_line == 0, lines - 1, 0)
    outer = picks((col == sent * RPL + (at_tm ^ d) * (half // lines) + spot) & (spot < half // lines))
    copy.wait()
    moved = jnp.dot(order, held[...], preferred_element_type=F32).astype(BF)
    edge = jnp.dot(outer, held[...], preferred_element_type=F32).astype(BF)
    outs[0][...] = moved[:half]
    outs[1][...] = moved[half:]
    outs[2][...] = edge[:16]
    outs[3][...] = edge[16:]


def places(plan, first):
    at_shot, at_line, at_tm = (lax.axis_index(a) for a in ("shot", "line", "tm"))
    if not plan.paired:
        return at_shot, at_tm * plan.lines, at_tm, at_shot, at_line
    return at_tm * (RPL // 2) + (0 if first else at_shot * plan.per), 0, at_tm, at_shot, at_line


def split_index(value, size):
    if size & (size - 1):
        return value // size, value % size
    return value >> (size.bit_length() - 1), value & (size - 1)


def section_map(plan, place, tallies, first):
    shape = (plan.rows, SLAB)
    lane = lax.broadcasted_iota(jnp.int32, shape, 1)
    apart, line = split_index(iota(shape, 0), plan.lines)
    if not first:
        apart = split_index(apart, plan.per)[1]
    spot = (line + place[1]) * RPL + place[0] + apart
    low = jnp.zeros(shape, jnp.int32)
    high = jnp.zeros(shape, jnp.int32)
    count = jnp.zeros(shape, jnp.int32)
    start = jnp.int32(0)
    for p in range(plan.sections):
        amount = tallies[p]
        here = lane == p
        low = jnp.where(here, start, low)
        high = jnp.where(here, start + amount, high)
        count = jnp.where(here, amount, count)
        start = start + amount
    member = (spot >= low) & (spot < high)
    return member, count


def shifted(values, by, ok, edge):
    return jnp.where(ok, pltpu.roll(values, by % values.shape[0], 0), edge)


def pack_inputs(plan, channels, packed):
    lane = lax.broadcasted_iota(jnp.int32, (plan.rows, SLAB), 1)
    low = lane < HALF
    ones = ((lane >= ONES - SLAB) & (lane < ONES - SLAB + 3)).astype(F32)
    slabs = [[x[:, t * SLAB : (t + 1) * SLAB] for t in range(plan.slabs)] for x in channels]
    far = [[pltpu.roll(s, HALF + 1 + 2 * c, 1) for s in slabs[c]] for c in range(3)]
    for t in range(plan.slabs):
        v = [slabs[c][t] for c in range(3)]
        w = [pltpu.roll(s, HALF, 1) for s in v]
        even = jnp.where(low, v[2], ones)
        odd = jnp.where(low, w[2], ones)
        for c in range(3):
            left, right = lane == HALF + 2 * c, lane == HALF + 2 * c + 1
            near = pltpu.roll(v[c], 1 + 2 * c, 1)
            even = jnp.where(right, near, even)
            odd = jnp.where(left, near, odd)
            if t > 0:
                even = jnp.where(left, far[c][t - 1], even)
            if t < plan.slabs - 1:
                odd = jnp.where(right, far[c][t + 1], odd)
        packed[0, t, :, 0:SLAB] = jnp.where(low, v[0], w[1]).astype(BF)
        packed[0, t, :, SLAB:WIDE] = even.astype(BF)
        packed[1, t, :, 0:SLAB] = jnp.where(low, w[0], v[1]).astype(BF)
        packed[1, t, :, SLAB:WIDE] = odd.astype(BF)


def network(plan, weights, scratch, regions):
    w_in, w_out = weights
    packed, hidden, total, ends = scratch
    slabs, rows = plan.slabs, plan.rows
    many = slabs * rows
    pitch = slabs + 2

    def first(q):
        taps = jnp.concatenate([w_in[q], w_in[q + 1]], axis=1)
        value = jnp.dot(packed[...].reshape(2 * many, WIDE), taps, preferred_element_type=F32)
        value = jnp.maximum(value.astype(BF), 0).reshape(2, slabs, rows, 2 * WIDE)
        for h in range(2):
            for k in range(2):
                at = pl.ds((q + k + h * QH) * pitch + 1, slabs)
                hidden[at] = value[h, :, :, k * WIDE : (k + 1) * WIDE]

    lane = iota((slabs, rows, SLAB), 2)
    ones = picks(lane < 3)

    def window(q):
        if isinstance(q, int):
            left_at = (q - 2) * pitch + 1 if q >= 2 else (q + QS - 2) * pitch
            right_at = (q + 2) * pitch + 1 if q < QS - 2 else (q + 2 - QS) * pitch + 2
        else:
            left_at = jnp.where(q >= 2, (q - 2) * pitch + 1, (q + QS - 2) * pitch)
            right_at = jnp.where(q < QS - 2, (q + 2) * pitch + 1, (q + 2 - QS) * pitch + 2)
        middle = hidden[pl.ds(q * pitch + 1, slabs)]
        left = hidden[pl.ds(left_at, slabs), :, SLAB:WIDE]
        right = hidden[pl.ds(right_at, slabs), :, 0:SLAB]
        beside = jnp.where(lane < FEAT, right, left)
        return jnp.concatenate([middle, beside, ones], axis=2).reshape(many, 2 * WIDE)

    def second(q):
        both = jnp.concatenate([window(q), window(q + 1)], axis=0)
        value = jnp.dot(both, w_in[QH:].reshape(2 * WIDE, WIDE), preferred_element_type=F32)
        value = jnp.maximum(value.astype(BF), 0)
        return value[:many], value[many:]

    def onto(layer, taps):
        return jnp.dot(layer, taps, preferred_element_type=F32).reshape(slabs, rows, SLAB)

    edge = jnp.zeros((rows, WIDE), BF)
    for k in range(2):
        hidden[(QS - 2 + k) * pitch] = edge
        hidden[(k + 1) * pitch - 1] = edge
    total[...] = jnp.zeros_like(total)

    @regions
    def _():
        for q in range(0, QH, 2):
            first(q)

    @regions
    def _():
        for q in range(0, QS, 2):
            one, two = second(q)
            total[...] += onto(jnp.concatenate([one, two], axis=1), w_out[q : q + 2].reshape(2 * WIDE, SLAB))
            if q == 0:
                ends[0] = one
            if q == QS - 2:
                ends[1] = two

    total[0 : slabs - 1] += onto(ends[0], w_out[QS + 1])[1:]
    total[1:slabs] += onto(ends[1], w_out[QS])[: slabs - 1]


def add_total(plan, now, total, scale=None):
    for t in range(plan.slabs):
        lanes = slice(t * SLAB, (t + 1) * SLAB)
        more = total[t] if scale is None else scale * total[t]
        now[:, lanes] = (now[:, lanes] + more).astype(BF).astype(F32)


def shot_stage(plan, place, tallies, first, edges, weights, now, scratch):
    apart = pl.when(place[0] >= 0)

    @apart
    def _():
        x = now[...]
        line = split_index(iota(x.shape, 0), plan.lines)[1]
        if plan.paired:
            wide = [jnp.broadcast_to(edges[g : g + 1, :], (plan.lines, x.shape[1])) for g in range(plan.groups)]
            wide = jnp.concatenate(wide, axis=0)
            above = jnp.where(place[4] == 1, wide, 0.0)
            below = jnp.where(place[4] == 1, 0.0, wide)
        else:
            above, below = edges[0].astype(F32), edges[1].astype(F32)
        channels = [
            shifted(x, 1, line > 0, above),
            x,
            shifted(x, -1, line < plan.lines - 1, below),
        ]
        pack_inputs(plan, channels, scratch[0])

    network(plan, weights, scratch, apart)
    add_total(plan, now, scratch[2])
    power = jnp.zeros((plan.rows, SLAB), F32)
    for t in range(plan.slabs):
        piece = now[:, t * SLAB : (t + 1) * SLAB]
        power = power + piece * piece
    member, _ = section_map(plan, place, tallies, first)
    each = jnp.where(member, jnp.sum(power, axis=1, keepdims=True), 0.0)
    return jnp.sum(each, axis=0, keepdims=True)


def station_stage(
    plan, place, tallies, lags, order, pace, energies, mixes, fetches, weights, now, scratch, blend
):
    fired, misfit, scale = blend
    apart = pl.when(place[0] >= 0)

    @apart
    def _():
        member, count = section_map(plan, place, tallies, False)
        denominator = jnp.maximum(count, 1) * (plan.shots * plan.slabs * SLAB)
        level = jnp.sqrt(energies[...] / denominator.astype(F32) + EPSILON)
        rms = jnp.sum(jnp.where(member, level, 0.0), axis=1, keepdims=True)
        scale[...] = jnp.broadcast_to(rms, scale.shape)
        x = (now[...] / rms).astype(BF).astype(F32)
        row = iota(x.shape, 0)
        channels = [
            shifted(x, plan.span, row >= plan.span, 0.0),
            x,
            shifted(x, -plan.span, row < plan.rows - plan.span, 0.0),
        ]
        pack_inputs(plan, channels, scratch[0])

    network(plan, weights, scratch, apart)
    add_total(plan, now, scratch[2], scale[...])
    lane = lax.broadcasted_iota(jnp.int32, (plan.span, SLAB), 1)
    mixtures = misfit.shape[0]
    per = plan.shots // mixtures
    if plan.paired:
        row, col = iota((plan.span, mixes.shape[1]), 0), iota((plan.span, mixes.shape[1]), 1)
        spot, line = split_index(row, plan.lines)
        choose = picks(col == line * RPL + place[0] + spot)
        for g in range(mixtures):
            fetches[g].wait()
            misfit[g] = jnp.dot(choose, mixes[g], preferred_element_type=F32)
    else:
        misfit[...] = mixes[...].astype(F32)
    for s in range(plan.shots):
        lag = lags[s]
        before = jnp.zeros((plan.span, SLAB), F32)
        for t in range(plan.slabs):
            lanes = slice(t * SLAB, (t + 1) * SLAB)
            turned = pltpu.roll(now[s * plan.span : (s + 1) * plan.span, lanes], lag, 1)
            fired[s, :, lanes] = jnp.where(lane < lag, before, turned)
            before = turned
    for g in range(mixtures):
        value = fired[order[g * per]]
        for k in range(1, per):
            value = value + fired[order[g * per + k]]
        misfit[g] = value - misfit[g]
    for s in range(plan.shots):
        lag = lags[s]
        spot = jnp.int32(0)
        for k in range(plan.shots):
            spot = spot + jnp.where(order[k] == s, k, 0)
        which = spot // per
        back = (DMAX - lag) % DMAX
        after = jnp.zeros((plan.span, SLAB), F32)
        rows = slice(s * plan.span, (s + 1) * plan.span)
        for t in range(plan.slabs - 1, -1, -1):
            lanes = slice(t * SLAB, (t + 1) * SLAB)
            turned = pltpu.roll(misfit[which, :, lanes], back, 1)
            pulled = jnp.where(lane < DMAX - lag, turned, after)
            after = turned
            now[rows, lanes] = (now[rows, lanes] - pace * pulled).astype(BF).astype(F32)


def stage_kernel(plan, station_round, with_shot, first, split_in, split_out, *refs):
    refs = list(refs)
    take = lambda n: [refs.pop(0) for _ in range(n)]
    tallies, lags, order, paces = take(4)
    place = places(plan, first)
    sources = take(4 if split_in else 1)
    station = station_round is not None
    if station:
        energies, mixes = take(2)
        station_weights = take(2)
    if with_shot:
        edges = take(0 if first else 1)
        shot_weights = take(2)
    results = take({"parts": plan.each, "edge": 2}.get(split_out, 1))
    if with_shot and split_out != "parts":
        (energy,) = take(1)
    now, packed, hidden, total, ends, rim = take(6)
    scratch = (packed, hidden, total, ends)
    length = plan.slabs * SLAB
    fetches = []
    if station and plan.paired:
        done, held = refs.pop(), refs.pop()
        fetches = [pltpu.make_async_copy(mixes.at[g], held.at[g], done.at[g]) for g in range(plan.mixtures)]
        for fetch in fetches:
            fetch.start()
        mixes = held
    if split_in == "parts":
        for d, part in enumerate(sources):
            at = pl.multiple_of((place[3] ^ d) * plan.span, plan.span)
            now[pl.ds(at, plan.span), :] = part[:, 0:length].astype(F32)
    elif split_in:
        share = length // plan.time_parts
        for d in range(2):
            lanes = pl.ds(pl.multiple_of((place[2] ^ d) * share, share), share)
            now[:, lanes] = sources[d][...].astype(F32)
            rim[:, lanes] = sources[2 + d][...].astype(F32)
    else:
        now[...] = sources[0][...].astype(F32)
    if station:
        station_stage(
            plan,
            place,
            tallies,
            lags,
            order,
            paces[station_round],
            energies,
            mixes,
            fetches,
            station_weights,
            now,
            scratch,
            refs,
        )
    if with_shot:
        if plan.paired and not first:
            rim[...] = edges[0][...].astype(F32)
        outer = rim if plan.paired else edges[0]
        sums = shot_stage(plan, place, tallies, first, outer, shot_weights, now, scratch)
    if split_out == "parts":
        row = iota((plan.span, SLAB), 0)
        beside = jnp.zeros((plan.span, SLAB), F32)
        for i, part in enumerate(split_bias(sums)):
            beside = jnp.where(row == i, part, beside)
        for d, part in enumerate(results):
            at = pl.multiple_of((place[3] ^ d) * plan.span, plan.span)
            part[:, 0:length] = now[pl.ds(at, plan.span), :].astype(BF)
            part[:, length:] = beside.astype(BF)
        return
    if with_shot:
        energy[...] = sums
    if split_out == "final":
        share = length // plan.time_parts
        for n in range(results[0].shape[0]):
            b, k = divmod(n, plan.each)
            results[0][n] = now[k * plan.span : (k + 1) * plan.span, b * share : (b + 1) * share].astype(BF)
        return
    results[0][...] = now[...].astype(BF)
    if split_out == "edge":
        row, col = iota((16, plan.rows), 0), iota((16, plan.rows), 1)
        sent = jnp.where(place[4] == 0, plan.lines - 1, 0)
        choose = picks(col == row * plan.lines + sent)
        results[1][...] = jnp.dot(choose, now[...].astype(BF), preferred_element_type=F32).astype(BF)


SMEM = pl.BlockSpec(memory_space=pltpu.SMEM)
VMEM = pl.BlockSpec(memory_space=pltpu.VMEM)
HBM = pl.BlockSpec(memory_space=pltpu.HBM)


def run_stage(plan, small, source, station=None, shot=None, first=False, split_in=None, split_out=None, name="stage"):
    operands = [*small, *source]
    specs = [SMEM] * len(small) + [VMEM] * len(source)
    station_round = None
    macs = 0
    pass_macs = plan.rows * plan.slabs * QS * WIDE * (WIDE * 3 + SLAB)
    if station is not None:
        station_round, energies, mixes, weights = station
        operands += [energies, mixes, *weights]
        specs += [VMEM, HBM if plan.paired else VMEM, VMEM, VMEM]
        macs += pass_macs
    if shot is not None:
        edges, weights = shot
        operands += [*edges, *weights]
        specs += [VMEM] * (len(edges) + 2)
        macs += pass_macs
    length = plan.slabs * SLAB
    if split_out == "parts":
        shapes = [jax.ShapeDtypeStruct((plan.span, length + SLAB), BF)] * plan.each
    elif split_out == "final":
        shapes = [jax.ShapeDtypeStruct((plan.each * plan.time_parts, plan.span, length // plan.time_parts), BF)]
    else:
        shapes = [jax.ShapeDtypeStruct((plan.rows, length), BF)]
        if split_out == "edge":
            shapes.append(jax.ShapeDtypeStruct((16, length), BF))
    if shot is not None and split_out != "parts":
        shapes.append(jax.ShapeDtypeStruct((1, SLAB), F32))
    scratch = [
        pltpu.VMEM((plan.rows, length), F32),
        pltpu.VMEM((2, plan.slabs, plan.rows, WIDE), BF),
        pltpu.VMEM((QS * (plan.slabs + 2), plan.rows, WIDE), BF),
        pltpu.VMEM((plan.slabs, plan.rows, SLAB), F32),
        pltpu.VMEM((2, plan.slabs * plan.rows, WIDE), BF),
        pltpu.VMEM((16, length), F32),
    ]
    if station is not None:
        scratch += [
            pltpu.VMEM((plan.shots, plan.span, length), F32),
            pltpu.VMEM((plan.mixtures, plan.span, length), F32),
            pltpu.VMEM((plan.rows, SLAB), F32),
        ]
        if plan.paired:
            scratch += [pltpu.VMEM(mixes.shape, BF), pltpu.SemaphoreType.DMA((plan.mixtures,))]
    return pl.pallas_call(
        functools.partial(stage_kernel, plan, station_round, shot is not None, first, split_in, split_out),
        out_shape=shapes,
        in_specs=specs,
        out_specs=[VMEM] * len(shapes),
        scratch_shapes=scratch,
        compiler_params=pltpu.CompilerParams(vmem_limit_bytes=VMEM_LIMIT),
        cost_estimate=pl.CostEstimate(flops=2 * macs, bytes_accessed=1 << 20, transcendentals=0),
        name=name,
    )(*operands)


def bundled(entry, spaced, leave):
    rows = [spaced.reshape(3 * FEAT, FEAT), jnp.pad(leave, ((0, 12), (0, 0)))]
    rows.append(jnp.pad(entry.transpose(1, 0, 2), ((0, 0), (0, 12), (0, 0))).reshape(48, FEAT))
    return jnp.concatenate(rows, axis=0)


def run_prepare(bundle, bias, name):
    return pl.pallas_call(
        prepare_kernel,
        out_shape=[
            jax.ShapeDtypeStruct((QH + 2, WIDE, WIDE), BF),
            jax.ShapeDtypeStruct((QS + 2, WIDE, SLAB), BF),
        ],
        in_specs=[VMEM] * 2,
        out_specs=[VMEM] * 2,
        scratch_shapes=[pltpu.VMEM((SLAB, WIDE), F32), pltpu.VMEM((SLAB, WIDE), F32)],
        compiler_params=pltpu.CompilerParams(vmem_limit_bytes=VMEM_LIMIT),
        cost_estimate=pl.CostEstimate(flops=2 * 8192 * WIDE * SLAB, bytes_accessed=4 << 20, transcendentals=0),
        name=name,
    )(bundle, bias)


def run_pack(plan, traces):
    block, width = traces.shape
    return pl.pallas_call(
        functools.partial(pack_kernel, plan),
        out_shape=[jax.ShapeDtypeStruct((rows, width), BF) for rows in (block // 2, block // 2, 16, 16)],
        in_specs=[HBM],
        out_specs=[VMEM] * 4,
        scratch_shapes=[pltpu.VMEM((block, width), BF), pltpu.SemaphoreType.DMA],
        compiler_params=pltpu.CompilerParams(vmem_limit_bytes=VMEM_FULL),
        cost_estimate=pl.CostEstimate(flops=2 * block * block * width, bytes_accessed=1 << 20, transcendentals=0),
        name="pack",
    )(traces)


class Plan:
    def __init__(self, **sizes):
        self.__dict__.update(sizes)
        self.span = self.lines * self.per
        self.rows = self.shots * self.span
        self.groups = self.rows // self.lines


def exchanged(parts, axes):
    size = len(parts)
    return [parts[0]] + [lax.ppermute(parts[d], axes, [(i, i ^ d) for i in range(size)]) for d in range(1, size)]


def per_device(
    initial_guess,
    measured_mixtures,
    launch_lags,
    source_launch_order,
    station_portion_tallies,
    source_entry_kernel,
    source_spaced_kernel,
    source_exit_kernel,
    source_inner_offsets,
    station_entry_kernel,
    station_spaced_kernel,
    station_exit_kernel,
    station_inner_offsets,
    learned_pace_factors,
):
    shots_here, block, window = initial_guess.shape
    n_shot, n_line, n_tm = (lax.axis_size(a) for a in ("shot", "line", "tm"))
    at_shot, at_tm = lax.axis_index("shot"), lax.axis_index("tm")
    block_lines = block // RPL
    length = window * n_tm
    shots = shots_here * n_shot
    sections = station_portion_tallies.shape[0]
    mixtures = measured_mixtures.shape[0]
    paired = n_shot * n_line * n_tm == RPL and n_line == 2 and n_tm == 2 and block_lines == 8
    assert shots_here == 1 and (paired or n_shot == RPL)
    plan = Plan(
        paired=paired,
        shots=shots,
        lines=block_lines if paired else block_lines // n_tm,
        per=RPL // (n_shot * n_tm) if paired else 1,
        sections=sections,
        mixtures=mixtures,
        slabs=length // SLAB,
        each=n_shot,
        time_parts=n_tm,
    )
    lines = plan.lines

    if paired:
        source = exchanged(run_pack(plan, initial_guess.reshape(block, window)), ("line", "tm"))
        mixes = measured_mixtures
    else:
        grid = initial_guess.reshape(n_tm, lines, RPL, window)
        leaving = grid.transpose(2, 0, 1, 3).reshape(RPL * n_tm, lines, window)
        arrived = lax.all_to_all(leaving, ("shot", "tm"), split_axis=0, concat_axis=0, tiled=True)
        source = arrived.reshape(n_shot, n_tm, lines, window).transpose(0, 2, 1, 3).reshape(plan.rows, length)
        grid = measured_mixtures.reshape(mixtures, n_tm, lines, RPL, length)
        mixes = lax.dynamic_slice(grid, (0, at_tm, 0, at_shot, 0), (mixtures, 1, lines, 1, length))
        mixes = mixes.reshape(mixtures, lines, length)

    shot_bundle = bundled(source_entry_kernel, source_spaced_kernel, source_exit_kernel)
    station_net = (station_entry_kernel, station_spaced_kernel, station_exit_kernel)
    shot_weights = run_prepare(shot_bundle, source_inner_offsets, "prepare_shot")
    small = (station_portion_tallies, launch_lags, source_launch_order, learned_pace_factors)
    def edges_of(current):
        size = n_line * n_tm
        grid = current.reshape(shots, lines, length)
        up = [(i, i + 1) for i in range(size - 1)]
        down = [(j, i) for i, j in up]
        above = lax.ppermute(grid[:, -1], ("line", "tm"), up)
        below = lax.ppermute(grid[:, 0], ("line", "tm"), down)
        wide = jnp.broadcast_to(jnp.stack([above, below])[:, :, None, :], (2, shots, lines, length))
        return wide.reshape(2, plan.rows, length)

    def summed(value, axis):
        size = lax.axis_size(axis)
        if size <= 4:
            others = [lax.ppermute(value, axis, [(i, i ^ d) for i in range(size)]) for d in range(1, size)]
            return sum(others, value)
        step = 1
        while step < size:
            value = value + lax.ppermute(value, axis, [(i, i ^ step) for i in range(size)])
            step *= 2
        return value

    def shared(energy, along):
        for axis in along:
            energy = summed(energy, axis)
        return energy

    if paired:
        parts = run_stage(
            plan,
            small,
            source,
            shot=([], shot_weights),
            first=True,
            split_in="packets",
            split_out="parts",
            name="shot_pass",
        )
        station_net, own = lax.optimization_barrier((station_net, parts[0]))
        current = exchanged([own, *parts[1:]], "shot")
        bundle = bundled(*station_net)
        station_weights = run_prepare(bundle, station_inner_offsets, "prepare_station")
        energy = sum(jnp.sum(p[0:3, length:].astype(F32), axis=0, keepdims=True) for p in current)
        station_weights, energy = lax.optimization_barrier((station_weights, energy))
        energy = summed(energy, "tm")
    else:
        current, energy = run_stage(plan, small, [source], shot=([edges_of(source)], shot_weights), name="shot_pass")
        energy = shared(energy, ("tm", "shot"))
        station_weights = run_prepare(bundled(*station_net), station_inner_offsets, "prepare_station")
    for i in range(ITERS):
        station = (i, energy, mixes, station_weights)
        form = {"split_in": "parts"} if paired and i == 0 else {}
        came = current if form else [current]
        if i == ITERS - 1:
            form["split_out"] = "final" if paired else None
            (current,) = run_stage(plan, small, came, station=station, name="station_pass", **form)
        elif paired:
            current, edge = run_stage(
                plan, small, came, station=station, name="station_pass", split_out="edge", **form
            )
            edge = lax.ppermute(edge, "line", [(0, 1), (1, 0)])
            current, energy = run_stage(plan, small, [current], shot=([edge], shot_weights), name="shot_pass")
            fresh, energy = lax.optimization_barrier((bundle, energy))
            station_weights = run_prepare(fresh, station_inner_offsets, "prepare_station")
            energy = shared(energy, ("tm", "shot"))
        else:
            (current,) = run_stage(plan, small, came, station=station, name="station_pass")
            edges = [edges_of(current)]
            current, energy = run_stage(plan, small, [current], shot=(edges, shot_weights), name="shot_pass")
            energy = shared(energy, ("tm", "shot"))
    if paired:
        back = lax.all_to_all(current, ("tm", "shot"), split_axis=0, concat_axis=0, tiled=True)
        back = back.reshape(RPL, lines, window).transpose(1, 0, 2)
    else:
        current = current.reshape(n_shot, lines, n_tm, window).transpose(0, 2, 1, 3).reshape(-1, lines, window)
        back = lax.all_to_all(current, ("shot", "tm"), split_axis=0, concat_axis=0, tiled=True)
        back = back.reshape(RPL, n_tm, lines, window).transpose(1, 2, 0, 3)
    return back.reshape(shots_here, block, window)


def solution(mesh):
    placed = (P(("group", "shot"), "line", "tm"), P("group", "line", None), P("group"), P("group"), P("group"))
    return jax.shard_map(
        per_device,
        mesh=mesh,
        in_specs=placed + (P(),) * 9,
        out_specs=P(("group", "shot"), "line", "tm"),
        check_vma=False,
    )
```

profile of v0, /device:TPU:0, one launch (start us, length us, event | category | flops | bytes accessed | tf_op | source)
XLA Modules:
  0.0 69.5 jit_solution(5718252621653469653)
XLA Ops:
  0.0 1.8 %pack.1 = (bf16[64,512]{1,0:T(8,128)(2,1)}, bf16[64,512]{1,0:T(8,128)(2,1)}, bf16[16,512]{1,0:T(8,128)(2,1)}, bf16[16,512]{1,0:T(8,128)(2,1)}) custom-call(bf16[128,512]{1,0:T(8,128)(2,1)} %bitcast.14), custom_call_target="tpu_custom_call" | custom-call | flops 16777216 | bytes 1048576 | tf_op jit(solution)/shard_map/pack/pallas_call | solution.py:526
  1.8 0.0 copy-start.1
  1.8 3.0 %collective-permute-start.1 = (bf16[16,512]{1,0:T(8,128)(2,1)}, bf16[16,512]{1,0:T(8,128)(2,1)S(1)}, u32[]{:S(2)}, u32[]{:S(2)}) collective-permute-start(bf16[16,512]{1,0:T(8,128)(2,1)} %get-tuple-element.34), channel_id=1, source_target_pairs={{0,2},{1,3},{2,0},{3,1},{4,6},{5,7},{6,4},{7,5},{8,10},{9,11},{10,... | collective-permute-start | bytes 49160 | tf_op jit(solution)/shard_map/ppermute | solution.py:548
  4.8 0.2 collective-permute-start
  5.0 0.7 pad.15
  5.7 0.8 %fusion.4.bundle = bf16[256,64]{1,0:T(8,128)(2,1)S(1)} fusion(bf16[4,64]{1,0:T(4,128)(2,1)} %param.21, bf16[48,64]{1,0:T(8,128)(2,1)S(1)} %bitcast.18, bf16[192,64]{1,0:T(8,128)(2,1)} %bitcast.15), kind=kLoop, calls=%fused_computation.6 | loop fusion | flops 163840 | bytes 64000 | tf_op jit(solution)/shard_map/concatenate | solution.py:505
  6.5 0.7 copy-done.2
  7.2 0.8 %prepare_shot.1 = (bf16[10,256,256]{2,1,0:T(8,128)(2,1)S(1)}, bf16[18,256,128]{2,1,0:T(8,128)(2,1)S(1)}) custom-call(bf16[256,64]{1,0:T(8,128)(2,1)S(1)} %fusion.4.bundle, f32[2,64]{1,0:T(2,128)S(1)} %copy-done.2), custom_call_target="tpu_custom_call" | custom-call | flops 536870912 | bytes 4194304 | tf_op jit(solution)/shard_map/prepare_shot/pallas_call | solution.py:509
  8.0 0.1 collective-permute-done.2.refs_7_
  8.3 0.0 copy-start.10
  8.3 6.4 %shot_pass.2 = (bf16[16,1152]{1,0:T(8,128)(2,1)S(1)}, bf16[16,1152]{1,0:T(8,128)(2,1)S(1)}, bf16[16,1152]{1,0:T(8,128)(2,1)S(1)}, bf16[16,1152]{1,0:T(8,128)(2,1)S(1)}) custom-call(s32[8]{0:T(128)S(1)} %copy-done.4, s32[4]{0:T(128)S(1)} %copy-done.5, s32[4]{0:T(128)S(1)} %copy-done.6, f32[2]{0:T(128)S(1)} %copy-done.7, bf16[64,512]{1,0:T(8,128)(2,1)S(1)} %copy-done.1, ...), custom_call_target="tpu_custom_call" | custom-call | flops 3758096384 | bytes 1048576 | tf_op jit(solution)/shard_map/shot_pass/pallas_call | solution.py:490
  14.8 2.0 %collective-permute-start.3 = (bf16[16,1152]{1,0:T(8,128)(2,1)S(1)}, bf16[16,1152]{1,0:T(8,128)(2,1)S(1)}, u32[]{:S(2)}, u32[]{:S(2)}) collective-permute-start(bf16[16,1152]{1,0:T(8,128)(2,1)S(1)} %get-tuple-element.40), channel_id=1, source_target_pairs={{0,4},{4,0},{8,12},{12,8},{1,5},{5,1},{9,13},{13,9},{2,6},{6,2},{1... | collective-permute-start | bytes 110600 | tf_op jit(solution)/shard_map/ppermute | solution.py:548
  16.7 2.6 %collective-permute-start.4 = (bf16[16,1152]{1,0:T(8,128)(2,1)S(1)}, bf16[16,1152]{1,0:T(8,128)(2,1)S(1)}, u32[]{:S(2)}, u32[]{:S(2)}) collective-permute-start(bf16[16,1152]{1,0:T(8,128)(2,1)S(1)} %get-tuple-element.41), channel_id=1, source_target_pairs={{0,8},{4,12},{8,0},{12,4},{1,9},{5,13},{9,1},{13,5},{2,10},{6,14},... | collective-permute-start | bytes 110600 | tf_op jit(solution)/shard_map/ppermute | solution.py:548
  19.4 0.8 %prepare_station.2 = (bf16[10,256,256]{2,1,0:T(8,128)(2,1)S(1)}, bf16[18,256,128]{2,1,0:T(8,128)(2,1)S(1)}) custom-call(bf16[256,64]{1,0:T(8,128)(2,1)S(1)} %fusion.6.bundle, f32[2,64]{1,0:T(2,128)S(1)} %copy-done.3), custom_call_target="tpu_custom_call" | custom-call | flops 536870912 | bytes 4194304 | tf_op jit(solution)/shard_map/prepare_station/pallas_call | solution.py:509
  20.2 2.1 %collective-permute-done.4.refs_6_ = bf16[16,1152]{1,0:T(8,128)(2,1)S(1)} collective-permute-done((bf16[16,1152]{1,0:T(8,128)(2,1)S(1)}, bf16[16,1152]{1,0:T(8,128)(2,1)S(1)}, u32[]{:S(2)}, u32[]{:S(2)}) %collective-permute-start.4) | collective-permute-done | bytes 36896 | tf_op jit(solution)/shard_map/ppermute | solution.py:548
  22.3 2.7 %collective-permute-done.5.refs_7_ = bf16[16,1152]{1,0:T(8,128)(2,1)S(1)} collective-permute-done((bf16[16,1152]{1,0:T(8,128)(2,1)S(1)}, bf16[16,1152]{1,0:T(8,128)(2,1)S(1)}, u32[]{:S(2)}, u32[]{:S(2)}) %collective-permute-start.5) | collective-permute-done | bytes 36896 | tf_op jit(solution)/shard_map/ppermute | solution.py:548
  25.1 0.1 collective-permute-start.6
  25.2 1.1 %collective-permute-done.6 = f32[1,128]{1,0:T(1,128)S(1)} collective-permute-done((f32[1,128]{1,0:T(1,128)S(1)}, f32[1,128]{1,0:T(1,128)S(1)}, u32[]{:S(2)}, u32[]{:S(2)}) %collective-permute-start.6) | collective-permute-done | bytes 544 | tf_op jit(solution)/shard_map/ppermute | solution.py:619
  26.3 7.3 %station_pass.2 = (bf16[64,1024]{1,0:T(8,128)(2,1)S(1)}, bf16[16,1024]{1,0:T(8,128)(2,1)S(1)}) custom-call(s32[8]{0:T(128)S(1)} %copy-done.4, s32[4]{0:T(128)S(1)} %copy-done.5, s32[4]{0:T(128)S(1)} %copy-done.6, f32[2]{0:T(128)S(1)} %copy-done.7, bf16[16,1152]{1,0:T(8,128)(2,1)S(1)} %get-tuple-element.39.refs_4_, ...), custom_call_target="tpu_custom_call" | custom-call | flops 3758096384 | bytes 1048576 | tf_op jit(solution)/shard_map/station_pass/pallas_call | solution.py:490
  33.6 1.6 %collective-permute-start.7 = (bf16[16,1024]{1,0:T(8,128)(2,1)S(1)}, bf16[16,1024]{1,0:T(8,128)(2,1)S(1)}, u32[]{:S(2)}, u32[]{:S(2)}) collective-permute-start(bf16[16,1024]{1,0:T(8,128)(2,1)S(1)} %get-tuple-element.52), channel_id=1, source_target_pairs={{0,2},{2,0},{1,3},{3,1},{4,6},{6,4},{5,7},{7,5},{8,10},{10,8},{9,1... | collective-permute-start | bytes 98312 | tf_op jit(solution)/shard_map/ppermute | solution.py:665
  35.2 2.4 %collective-permute-done.7.refs_5_ = bf16[16,1024]{1,0:T(8,128)(2,1)S(1)} collective-permute-done((bf16[16,1024]{1,0:T(8,128)(2,1)S(1)}, bf16[16,1024]{1,0:T(8,128)(2,1)S(1)}, u32[]{:S(2)}, u32[]{:S(2)}) %collective-permute-start.7) | collective-permute-done | bytes 32800 | tf_op jit(solution)/shard_map/ppermute | solution.py:665
  37.6 6.4 %shot_pass.3 = (bf16[64,1024]{1,0:T(8,128)(2,1)S(1)}, f32[1,128]{1,0:T(1,128)S(1)}) custom-call(s32[8]{0:T(128)S(1)} %copy-done.4, s32[4]{0:T(128)S(1)} %copy-done.5, s32[4]{0:T(128)S(1)} %copy-done.6, f32[2]{0:T(128)S(1)} %copy-done.7, bf16[64,1024]{1,0:T(8,128)(2,1)S(1)} %get-tuple-element.51.refs_4_, bf16[16,1024]{1,0:T(8,128)(2,1)S(1)} %collective-permute-done.7.refs_5_, ...), custom_call_target="tpu_custom_call" | custom-call | flops 3758096384 | bytes 1048576 | tf_op jit(solution)/shard_map/shot_pass/pallas_call | solution.py:490
  44.0 0.1 collective-permute-start.8
  44.1 1.1 %collective-permute-done.8 = f32[1,128]{1,0:T(1,128)S(1)} collective-permute-done((f32[1,128]{1,0:T(1,128)S(1)}, f32[1,128]{1,0:T(1,128)S(1)}, u32[]{:S(2)}, u32[]{:S(2)}) %collective-permute-start.8) | collective-permute-done | bytes 544 | tf_op jit(solution)/shard_map/ppermute | solution.py:619
  45.2 0.4 collective-permute-start.11
  45.7 3.9 %collective-permute-start.9 = (f32[1,128]{1,0:T(1,128)S(1)}, f32[1,128]{1,0:T(1,128)S(1)}, u32[]{:S(2)}, u32[]{:S(2)}) collective-permute-start(f32[1,128]{1,0:T(1,128)S(1)} %add.66), channel_id=1, source_target_pairs={{0,4},{4,0},{8,12},{12,8},{1,5},{5,1},{9,13},{13,9},{2,6},{6,2},{1... | collective-permute-start | bytes 1544 | tf_op jit(solution)/shard_map/ppermute | solution.py:619
  49.6 0.8 %prepare_station.3 = (bf16[10,256,256]{2,1,0:T(8,128)(2,1)S(1)}, bf16[18,256,128]{2,1,0:T(8,128)(2,1)S(1)}) custom-call(bf16[256,64]{1,0:T(8,128)(2,1)S(1)} %fusion.6.bundle, f32[2,64]{1,0:T(2,128)S(1)} %copy-done.3), custom_call_target="tpu_custom_call" | custom-call | flops 536870912 | bytes 4194304 | tf_op jit(solution)/shard_map/prepare_station/pallas_call | solution.py:509
  50.4 0.1 collective-permute-done.11
  50.6 0.6 collective-permute-done.9
  51.1 7.2 %station_pass.3 = bf16[8,16,512]{2,1,0:T(8,128)(2,1)S(1)} custom-call(s32[8]{0:T(128)S(1)} %copy-done.4, s32[4]{0:T(128)S(1)} %copy-done.5, s32[4]{0:T(128)S(1)} %copy-done.6, f32[2]{0:T(128)S(1)} %copy-done.7, bf16[64,1024]{1,0:T(8,128)(2,1)S(1)} %get-tuple-element.53.refs_4_, f32[1,128]{1,0:T(1,128)S(1)} %add_add_fusion.refs_5_, ...), custom_call_target="tpu_custom_call" | custom-call | flops 3758096384 | bytes 1048576 | tf_op jit(solution)/shard_map/station_pass/pallas_call | solution.py:490
  58.4 10.4 %all_to_all.5 = bf16[8,16,512]{2,1,0:T(8,128)(2,1)S(1)} all-to-all(bf16[8,16,512]{2,1,0:T(8,128)(2,1)S(1)} %station_pass.3), channel_id=1, replica_groups=mesh['group'=2,'shot'=4,'line'=2,'tm'=2] {'tm','shot'}, dimensions={0} | all-to-all | bytes 262144 | tf_op jit(solution)/shard_map/all_to_all | solution.py:676
  68.8 0.7 %copy.15 = bf16[8,16,512]{2,1,0:T(8,128)(2,1)} copy(bf16[8,16,512]{2,0,1:T(8,128)(2,1)S(1)} %bitcast.13) | data formatting | bytes 262144 | tf_op jit(solution)/shard_map/transpose | solution.py:677
  (36 shorter events, 0.2 us)
Async XLA Ops:
  0.0 8.2 %copy-start.7 = (f32[2]{0:T(128)S(1)}, f32[2]{0:T(128)}, u32[]{:S(2)}) copy-start(f32[2]{0:T(128)} %refs_3_.7) | copy-start | bytes 28
  0.0 8.2 %copy-start.4 = (s32[8]{0:T(128)S(1)}, s32[8]{0:T(128)}, u32[]{:S(2)}) copy-start(s32[8]{0:T(128)} %refs_0_.7) | copy-start | bytes 100
  0.0 8.2 %copy-start.6 = (s32[4]{0:T(128)S(1)}, s32[4]{0:T(128)}, u32[]{:S(2)}) copy-start(s32[4]{0:T(128)} %refs_2_.7) | copy-start | bytes 52
  0.0 8.2 %copy-start.5 = (s32[4]{0:T(128)S(1)}, s32[4]{0:T(128)}, u32[]{:S(2)}) copy-start(s32[4]{0:T(128)} %refs_1_.7) | copy-start | bytes 52
  1.8 6.4 %copy-start.1 = (bf16[64,512]{1,0:T(8,128)(2,1)S(1)}, bf16[64,512]{1,0:T(8,128)(2,1)}, u32[]{:S(2)}) copy-start(bf16[64,512]{1,0:T(8,128)(2,1)} %get-tuple-element.32.refs_4_) | copy-start | bytes 196612
  1.8 6.2 %collective-permute-start.1 = (bf16[16,512]{1,0:T(8,128)(2,1)}, bf16[16,512]{1,0:T(8,128)(2,1)S(1)}, u32[]{:S(2)}, u32[]{:S(2)}) collective-permute-start(bf16[16,512]{1,0:T(8,128)(2,1)} %get-tuple-element.34), channel_id=1, source_target_pairs={{0,2},{1,3},{2,0},{3,1},{4,6},{5,7},{6,4},{7,5},{8,10},{9,11},{10,... | collective-permute-start | bytes 49160 | tf_op jit(solution)/shard_map/ppermute | solution.py:548
  4.8 3.4 %collective-permute-start.2 = (bf16[16,512]{1,0:T(8,128)(2,1)}, bf16[16,512]{1,0:T(8,128)(2,1)S(1)}, u32[]{:S(2)}, u32[]{:S(2)}) collective-permute-start(bf16[16,512]{1,0:T(8,128)(2,1)} %get-tuple-element.35), channel_id=1, source_target_pairs={{0,3},{1,2},{2,1},{3,0},{4,7},{5,6},{6,5},{7,4},{8,11},{9,10},{10,... | collective-permute-start | bytes 49160 | tf_op jit(solution)/shard_map/ppermute | solution.py:548
  4.8 3.4 %collective-permute-start = (bf16[64,512]{1,0:T(8,128)(2,1)}, bf16[64,512]{1,0:T(8,128)(2,1)S(1)}, u32[]{:S(2)}, u32[]{:S(2)}) collective-permute-start(bf16[64,512]{1,0:T(8,128)(2,1)} %get-tuple-element.33), channel_id=1, source_target_pairs={{0,1},{1,0},{2,3},{3,2},{4,5},{5,4},{6,7},{7,6},{8,9},{9,8},{10,11... | collective-permute-start | bytes 196616 | tf_op jit(solution)/shard_map/ppermute | solution.py:548
  6.5 0.7 copy-start.2
  8.2 6.5 %copy-start.9 = (bf16[4,3,64]{2,0,1:T(4,128)(2,1)S(1)}, bf16[4,3,64]{2,0,1:T(4,128)(2,1)}, u32[]{:S(2)}) copy-start(bf16[4,3,64]{2,0,1:T(4,128)(2,1)} %param.23) | copy-start | bytes 4612
  8.2 11.1 %copy-start.8 = (bf16[3,64,64]{2,1,0:T(8,128)(2,1)S(1)}, bf16[3,64,64]{2,1,0:T(8,128)(2,1)}, u32[]{:S(2)}) copy-start(bf16[3,64,64]{2,1,0:T(8,128)(2,1)} %param.24) | copy-start | bytes 73732
  8.3 11.1 %copy-start.10 = (bf16[4,64]{1,0:T(4,128)(2,1)S(1)}, bf16[4,64]{1,0:T(4,128)(2,1)}, u32[]{:S(2)}) copy-start(bf16[4,64]{1,0:T(4,128)(2,1)} %param.25) | copy-start | bytes 1540
  8.3 11.1 %copy-start.3 = (f32[2,64]{1,0:T(2,128)S(1)}, f32[2,64]{1,0:T(2,128)}, u32[]{:S(2)}) copy-start(f32[2,64]{1,0:T(2,128)} %bias.5) | copy-start | bytes 1540
  14.7 11.6 %copy-start = (bf16[2,128,1024]{2,1,0:T(8,128)(2,1)S(1)}, bf16[2,128,1024]{2,1,0:T(8,128)(2,1)}, u32[]{:S(2)}) copy-start(bf16[2,128,1024]{2,1,0:T(8,128)(2,1)} %refs_6_.1) | copy-start | bytes 1572868
  14.8 5.4 %collective-permute-start.3 = (bf16[16,1152]{1,0:T(8,128)(2,1)S(1)}, bf16[16,1152]{1,0:T(8,128)(2,1)S(1)}, u32[]{:S(2)}, u32[]{:S(2)}) collective-permute-start(bf16[16,1152]{1,0:T(8,128)(2,1)S(1)} %get-tuple-element.40), channel_id=1, source_target_pairs={{0,4},{4,0},{8,12},{12,8},{1,5},{5,1},{9,13},{13,9},{2,6},{6,2},{1... | collective-permute-start | bytes 110600 | tf_op jit(solution)/shard_map/ppermute | solution.py:548
  16.7 5.6 %collective-permute-start.4 = (bf16[16,1152]{1,0:T(8,128)(2,1)S(1)}, bf16[16,1152]{1,0:T(8,128)(2,1)S(1)}, u32[]{:S(2)}, u32[]{:S(2)}) collective-permute-start(bf16[16,1152]{1,0:T(8,128)(2,1)S(1)} %get-tuple-element.41), channel_id=1, source_target_pairs={{0,8},{4,12},{8,0},{12,4},{1,9},{5,13},{9,1},{13,5},{2,10},{6,14},... | collective-permute-start | bytes 110600 | tf_op jit(solution)/shard_map/ppermute | solution.py:548
  19.3 5.8 %collective-permute-start.5 = (bf16[16,1152]{1,0:T(8,128)(2,1)S(1)}, bf16[16,1152]{1,0:T(8,128)(2,1)S(1)}, u32[]{:S(2)}, u32[]{:S(2)}) collective-permute-start(bf16[16,1152]{1,0:T(8,128)(2,1)S(1)} %get-tuple-element.42), channel_id=1, source_target_pairs={{0,12},{4,8},{8,4},{12,0},{1,13},{5,9},{9,5},{13,1},{2,14},{6,10},... | collective-permute-start | bytes 110600 | tf_op jit(solution)/shard_map/ppermute | solution.py:548
  25.1 1.2 %collective-permute-start.6 = (f32[1,128]{1,0:T(1,128)S(1)}, f32[1,128]{1,0:T(1,128)S(1)}, u32[]{:S(2)}, u32[]{:S(2)}) collective-permute-start(f32[1,128]{1,0:T(1,128)S(1)} %add_bitcast_fusion), channel_id=1, source_target_pairs={{0,1},{1,0},{2,3},{3,2},{4,5},{5,4},{6,7},{7,6},{8,9},{9,8},{10,11... | collective-permute-start | bytes 1544 | tf_op jit(solution)/shard_map/ppermute | solution.py:619
  33.6 4.0 %collective-permute-start.7 = (bf16[16,1024]{1,0:T(8,128)(2,1)S(1)}, bf16[16,1024]{1,0:T(8,128)(2,1)S(1)}, u32[]{:S(2)}, u32[]{:S(2)}) collective-permute-start(bf16[16,1024]{1,0:T(8,128)(2,1)S(1)} %get-tuple-element.52), channel_id=1, source_target_pairs={{0,2},{2,0},{1,3},{3,1},{4,6},{6,4},{5,7},{7,5},{8,10},{10,8},{9,1... | collective-permute-start | bytes 98312 | tf_op jit(solution)/shard_map/ppermute | solution.py:665
  44.0 1.2 %collective-permute-start.8 = (f32[1,128]{1,0:T(1,128)S(1)}, f32[1,128]{1,0:T(1,128)S(1)}, u32[]{:S(2)}, u32[]{:S(2)}) collective-permute-start(f32[1,128]{1,0:T(1,128)S(1)} %get-tuple-element.55), channel_id=1, source_target_pairs={{0,1},{1,0},{2,3},{3,2},{4,5},{5,4},{6,7},{7,6},{8,9},{9,8},{10,11... | collective-permute-start | bytes 1544 | tf_op jit(solution)/shard_map/ppermute | solution.py:619
  45.2 5.3 %collective-permute-start.11 = (f32[1,128]{1,0:T(1,128)S(1)}, f32[1,128]{1,0:T(1,128)S(1)}, u32[]{:S(2)}, u32[]{:S(2)}) collective-permute-start(f32[1,128]{1,0:T(1,128)S(1)} %add.66), channel_id=1, source_target_pairs={{0,12},{4,8},{8,4},{12,0},{1,13},{5,9},{9,5},{13,1},{2,14},{6,10},... | collective-permute-start | bytes 1544 | tf_op jit(solution)/shard_map/ppermute | solution.py:619
  45.7 4.9 %collective-permute-start.10 = (f32[1,128]{1,0:T(1,128)S(1)}, f32[1,128]{1,0:T(1,128)S(1)}, u32[]{:S(2)}, u32[]{:S(2)}) collective-permute-start(f32[1,128]{1,0:T(1,128)S(1)} %add.66), channel_id=1, source_target_pairs={{0,8},{4,12},{8,0},{12,4},{1,9},{5,13},{9,1},{13,5},{2,10},{6,14},... | collective-permute-start | bytes 1544 | tf_op jit(solution)/shard_map/ppermute | solution.py:619
  45.7 5.5 %collective-permute-start.9 = (f32[1,128]{1,0:T(1,128)S(1)}, f32[1,128]{1,0:T(1,128)S(1)}, u32[]{:S(2)}, u32[]{:S(2)}) collective-permute-start(f32[1,128]{1,0:T(1,128)S(1)} %add.66), channel_id=1, source_target_pairs={{0,4},{4,0},{8,12},{12,8},{1,5},{5,1},{9,13},{13,9},{2,6},{6,2},{1... | collective-permute-start | bytes 1544 | tf_op jit(solution)/shard_map/ppermute | solution.py:619
where the time goes:
time: 69.7 us; the launch traced here: 69.5 us
  Pallas kernels  31.6 us (45%)
  starting transfers between devices  13.9 us (20%)
  blocking collectives  10.4 us (15%)
  waiting for transfers between devices  10.3 us (15%)
  local copies, waits for them, and re-layouts  2.12 us (3%)
  other arithmetic  0.94 us (1%)
    pallas_call x4, Pallas kernels, run_stage(): pl.pallas_call(functools.partial(stage_kernel, plan, station_round, shot...  27.4 us
    all_to_all x1, blocking collectives, per_device(): lax.all_to_all(current, ('tm', 'shot'), split_axis=0, concat_axis=0, tile...  10.4 us
    ppermute x6, starting transfers between devices, exchanged(): lax.ppermute(parts[d], axes, [(i, i ^ d) for i in range(size)])  7.78 us
    ppermute x6, waiting for transfers between devices, exchanged(): lax.ppermute(parts[d], axes, [(i, i ^ d) for i in range(size)])  5 us
    ppermute x5, starting transfers between devices, summed(): lax.ppermute(value, axis, [(i, i ^ d) for i in range(size)])  4.53 us
    ppermute x5, waiting for transfers between devices, summed(): lax.ppermute(value, axis, [(i, i ^ d) for i in range(size)])  2.92 us
    ppermute x1, waiting for transfers between devices, per_device(): edge = lax.ppermute(edge, 'line', [(0, 1), (1, 0)])  2.43 us
    pallas_call x3, Pallas kernels, run_prepare(): pl.pallas_call(prepare_kernel, out_shape=[jax.ShapeDtypeStruct((QH + 2, W...  2.42 us
  transfers between devices with their start and end apart: 12, of which 8 were waited for; matrix products, arithmetic and copies ran while one was open for 2% of the time, Pallas kernels for 3%

commit v1 on v0

--- a/solution.py
+++ b/solution.py
@@ -46,16 +46,18 @@
     return 16 * (q // 2) + 2 * (q % 2)
 
 
-def prepare_kernel(bundle, bias, o_in, o_out, rhs, cols):
+def prepare_kernel(bundle, o_in, o_out, rhs, cols):
     rhs[...] = jnp.zeros_like(rhs)
     cols[...] = jnp.zeros_like(cols)
+    base = 3 * FEAT
+    bias = bundle[base + 16 : base + 24, :]
     parts = split_bias(bias[0:1, :])
-    exits = bundle[3 * FEAT : 3 * FEAT + 16, :].astype(F32)[0:4]
+    exits = bundle[base : base + 4, :]
     for p in range(GROUP):
         lanes = slice(p * FEAT, (p + 1) * FEAT)
         for c in range(3):
-            row = 3 * FEAT + 16 * (c + 1)
-            rhs[p * 32 + c * 8 : p * 32 + c * 8 + 4, lanes] = bundle[row : row + 16, :].astype(F32)[0:4]
+            row = base + 4 * (c + 1)
+            rhs[p * 32 + c * 8 : p * 32 + c * 8 + 4, lanes] = bundle[row : row + 4, :]
             rhs[p * 32 + 24 + c : p * 32 + 25 + c, lanes] = parts[c]
         cols[p * 8 : p * 8 + 4, lanes] = exits
     taps = rhs[...].astype(BF)
@@ -75,7 +77,7 @@
             if abs(a - b) <= 1:
                 tap = a - b + 1
                 rows, lanes = slice(at % 4 * FEAT, (at % 4 + 1) * FEAT), slice(b * FEAT, (b + 1) * FEAT)
-                o_in[QH + at // 4, rows, lanes] = bundle[tap * FEAT : (tap + 1) * FEAT, :]
+                o_in[QH + at // 4, rows, lanes] = bundle[tap * FEAT : (tap + 1) * FEAT, :].astype(BF)
     row = iota((16, FEAT), 0)
     below = jnp.zeros((16, FEAT), F32)
     for i, part in enumerate(split_bias(bias[1:2, :])):
@@ -93,12 +95,14 @@
         o_out[q] = jnp.dot(back, chosen, preferred_element_type=F32).astype(BF)
 
 
-def pack_kernel(plan, traces, *refs):
-    outs, held, done = refs[:4], refs[4], refs[5]
+def pack_kernel(plan, *refs):
+    sources, outs, fetched, done = refs[:9], refs[9:15], refs[15:24], refs[24]
+    held = fetched[0]
     _, _, at_tm, _, at_line = places(plan, True)
-    block = traces.shape[0]
-    copy = pltpu.make_async_copy(traces, held, done)
-    copy.start()
+    block = held.shape[0]
+    copies = [pltpu.make_async_copy(src, dst, done.at[i]) for i, (src, dst) in enumerate(zip(sources, fetched))]
+    for copy in copies:
+        copy.start()
     lines = plan.lines
     half = block // 2
     row, col = iota((block, block), 0), iota((block, block), 1)
@@ -109,13 +113,32 @@
     d, spot = split_index(row, 16)
     sent = jnp.where(at_line == 0, lines - 1, 0)
     outer = picks((col == sent * RPL + (at_tm ^ d) * (half // lines) + spot) & (spot < half // lines))
-    copy.wait()
+    for copy in copies:
+        copy.wait()
     moved = jnp.dot(order, held[...], preferred_element_type=F32).astype(BF)
     edge = jnp.dot(outer, held[...], preferred_element_type=F32).astype(BF)
     outs[0][...] = moved[:half]
     outs[1][...] = moved[half:]
     outs[2][...] = edge[:16]
     outs[3][...] = edge[16:]
+    for n, bundle in enumerate(outs[4:6]):
+        entry, spaced, leave, bias = fetched[1 + 4 * n : 5 + 4 * n]
+        for j in range(3):
+            bundle[j * FEAT : (j + 1) * FEAT, :] = spaced[j].astype(F32)
+            row = 3 * FEAT + 4 * (j + 1)
+            bundle[row : row + 4, :] = entry[j].astype(F32)
+        bundle[3 * FEAT : 3 * FEAT + 4, :] = leave[...].astype(F32)
+        bundle[3 * FEAT + 16 : 3 * FEAT + 24, :] = jnp.zeros((8, FEAT), F32)
+        bundle[3 * FEAT + 16 : 3 * FEAT + 18, :] = bias[...]
+
+
+def pick_kernel(plan, mixes, picked):
+    base = places(plan, False)[0]
+    row, col = iota((plan.span, mixes.shape[1]), 0), iota((plan.span, mixes.shape[1]), 1)
+    spot, line = split_index(row, plan.lines)
+    choose = picks(col == line * RPL + base + spot)
+    for g in range(plan.mixtures):
+        picked[g] = jnp.dot(choose, mixes[g], preferred_element_type=F32).astype(BF)
 
 
 def places(plan, first):
@@ -289,10 +312,10 @@
 
 
 def station_stage(
-    plan, place, tallies, lags, order, pace, energies, mixes, fetches, weights, now, scratch, blend
+    plan, place, tallies, lags, order, pace, energies, mixes, weights, now, scratch, blend
 ):
     fired, misfit, scale = blend
-    apart = pl.when(place[0] >= 0)
+    apart = lambda body: body()
 
     @apart
     def _():
@@ -315,15 +338,7 @@
     lane = lax.broadcasted_iota(jnp.int32, (plan.span, SLAB), 1)
     mixtures = misfit.shape[0]
     per = plan.shots // mixtures
-    if plan.paired:
-        row, col = iota((plan.span, mixes.shape[1]), 0), iota((plan.span, mixes.shape[1]), 1)
-        spot, line = split_index(row, plan.lines)
-        choose = picks(col == line * RPL + place[0] + spot)
-        for g in range(mixtures):
-            fetches[g].wait()
-            misfit[g] = jnp.dot(choose, mixes[g], preferred_element_type=F32)
-    else:
-        misfit[...] = mixes[...].astype(F32)
+    misfit[...] = mixes[...].astype(F32)
     for s in range(plan.shots):
         lag = lags[s]
         before = jnp.zeros((plan.span, SLAB), F32)
@@ -373,13 +388,6 @@
     now, packed, hidden, total, ends, rim = take(6)
     scratch = (packed, hidden, total, ends)
     length = plan.slabs * SLAB
-    fetches = []
-    if station and plan.paired:
-        done, held = refs.pop(), refs.pop()
-        fetches = [pltpu.make_async_copy(mixes.at[g], held.at[g], done.at[g]) for g in range(plan.mixtures)]
-        for fetch in fetches:
-            fetch.start()
-        mixes = held
     if split_in == "parts":
         for d, part in enumerate(sources):
             at = pl.multiple_of((place[3] ^ d) * plan.span, plan.span)
@@ -402,7 +410,6 @@
             paces[station_round],
             energies,
             mixes,
-            fetches,
             station_weights,
             now,
             scratch,
@@ -453,7 +460,7 @@
     if station is not None:
         station_round, energies, mixes, weights = station
         operands += [energies, mixes, *weights]
-        specs += [VMEM, HBM if plan.paired else VMEM, VMEM, VMEM]
+        specs += [VMEM] * 4
         macs += pass_macs
     if shot is not None:
         edges, weights = shot
@@ -485,8 +492,6 @@
             pltpu.VMEM((plan.mixtures, plan.span, length), F32),
             pltpu.VMEM((plan.rows, SLAB), F32),
         ]
-        if plan.paired:
-            scratch += [pltpu.VMEM(mixes.shape, BF), pltpu.SemaphoreType.DMA((plan.mixtures,))]
     return pl.pallas_call(
         functools.partial(stage_kernel, plan, station_round, shot is not None, first, split_in, split_out),
         out_shape=shapes,
@@ -499,40 +504,56 @@
     )(*operands)
 
 
-def bundled(entry, spaced, leave):
-    rows = [spaced.reshape(3 * FEAT, FEAT), jnp.pad(leave, ((0, 12), (0, 0)))]
-    rows.append(jnp.pad(entry.transpose(1, 0, 2), ((0, 0), (0, 12), (0, 0))).reshape(48, FEAT))
-    return jnp.concatenate(rows, axis=0)
-
-
-def run_prepare(bundle, bias, name):
+def bundled(entry, spaced, leave, bias):
+    rows = [spaced.reshape(3 * FEAT, FEAT), leave, entry.transpose(1, 0, 2).reshape(12, FEAT), bias]
+    return jnp.concatenate([r.astype(F32) for r in rows] + [jnp.zeros((6, FEAT), F32)], axis=0)
+
+
+def run_prepare(bundle, name):
     return pl.pallas_call(
         prepare_kernel,
         out_shape=[
             jax.ShapeDtypeStruct((QH + 2, WIDE, WIDE), BF),
             jax.ShapeDtypeStruct((QS + 2, WIDE, SLAB), BF),
         ],
-        in_specs=[VMEM] * 2,
+        in_specs=[VMEM],
         out_specs=[VMEM] * 2,
         scratch_shapes=[pltpu.VMEM((SLAB, WIDE), F32), pltpu.VMEM((SLAB, WIDE), F32)],
         compiler_params=pltpu.CompilerParams(vmem_limit_bytes=VMEM_LIMIT),
         cost_estimate=pl.CostEstimate(flops=2 * 8192 * WIDE * SLAB, bytes_accessed=4 << 20, transcendentals=0),
         name=name,
-    )(bundle, bias)
-
-
-def run_pack(plan, traces):
+    )(bundle)
+
+
+def run_pack(plan, traces, *nets):
     block, width = traces.shape
+    operands = [traces]
+    for entry, spaced, leave, bias in nets:
+        operands += [entry.transpose(1, 0, 2), spaced, leave, bias]
+    shapes = [jax.ShapeDtypeStruct((rows, width), BF) for rows in (block // 2, block // 2, 16, 16)]
+    shapes += [jax.ShapeDtypeStruct((3 * FEAT + 24, FEAT), F32)] * len(nets)
     return pl.pallas_call(
         functools.partial(pack_kernel, plan),
-        out_shape=[jax.ShapeDtypeStruct((rows, width), BF) for rows in (block // 2, block // 2, 16, 16)],
-        in_specs=[HBM],
-        out_specs=[VMEM] * 4,
-        scratch_shapes=[pltpu.VMEM((block, width), BF), pltpu.SemaphoreType.DMA],
+        out_shape=shapes,
+        in_specs=[HBM] * len(operands),
+        out_specs=[VMEM] * len(shapes),
+        scratch_shapes=[*(pltpu.VMEM(o.shape, o.dtype) for o in operands), pltpu.SemaphoreType.DMA((len(operands),))],
         compiler_params=pltpu.CompilerParams(vmem_limit_bytes=VMEM_FULL),
         cost_estimate=pl.CostEstimate(flops=2 * block * block * width, bytes_accessed=1 << 20, transcendentals=0),
         name="pack",
-    )(traces)
+    )(*operands)
+
+
+def run_pick(plan, mixes):
+    return pl.pallas_call(
+        functools.partial(pick_kernel, plan),
+        out_shape=jax.ShapeDtypeStruct((plan.mixtures, plan.span, mixes.shape[2]), BF),
+        in_specs=[VMEM],
+        out_specs=VMEM,
+        compiler_params=pltpu.CompilerParams(vmem_limit_bytes=VMEM_LIMIT),
+        cost_estimate=pl.CostEstimate(flops=1 << 24, bytes_accessed=1 << 20, transcendentals=0),
+        name="pick",
+    )(mixes)
 
 
 class Plan:
@@ -545,7 +566,8 @@
 
 def exchanged(parts, axes):
     size = len(parts)
-    return [parts[0]] + [lax.ppermute(parts[d], axes, [(i, i ^ d) for i in range(size)]) for d in range(1, size)]
+    came = [lax.ppermute(parts[d], axes, [(i, i ^ d) for i in range(size)]) for d in range(size - 1, 0, -1)]
+    return [parts[0]] + came[::-1]
 
 
 def per_device(
@@ -587,8 +609,11 @@
     )
     lines = plan.lines
 
+    shot_net = (source_entry_kernel, source_spaced_kernel, source_exit_kernel, source_inner_offsets)
+    station_net = (station_entry_kernel, station_spaced_kernel, station_exit_kernel, station_inner_offsets)
     if paired:
-        source = exchanged(run_pack(plan, initial_guess.reshape(block, window)), ("line", "tm"))
+        *source, shot_net, station_net = run_pack(plan, initial_guess.reshape(block, window), shot_net, station_net)
+        source = exchanged(source, ("line", "tm"))
         mixes = measured_mixtures
     else:
         grid = initial_guess.reshape(n_tm, lines, RPL, window)
@@ -598,10 +623,9 @@
         grid = measured_mixtures.reshape(mixtures, n_tm, lines, RPL, length)
         mixes = lax.dynamic_slice(grid, (0, at_tm, 0, at_shot, 0), (mixtures, 1, lines, 1, length))
         mixes = mixes.reshape(mixtures, lines, length)
-
-    shot_bundle = bundled(source_entry_kernel, source_spaced_kernel, source_exit_kernel)
-    station_net = (station_entry_kernel, station_spaced_kernel, station_exit_kernel)
-    shot_weights = run_prepare(shot_bundle, source_inner_offsets, "prepare_shot")
+        shot_net, station_net = bundled(*shot_net), bundled(*station_net)
+
+    shot_weights = run_prepare(shot_net, "prepare_shot")
     small = (station_portion_tallies, launch_lags, source_launch_order, learned_pace_factors)
     def edges_of(current):
         size = n_line * n_tm
@@ -640,17 +664,17 @@
             split_out="parts",
             name="shot_pass",
         )
-        station_net, own = lax.optimization_barrier((station_net, parts[0]))
+        station_net, mixes, own = lax.optimization_barrier((station_net, mixes, parts[0]))
         current = exchanged([own, *parts[1:]], "shot")
-        bundle = bundled(*station_net)
-        station_weights = run_prepare(bundle, station_inner_offsets, "prepare_station")
+        station_weights = run_prepare(station_net, "prepare_station")
         energy = sum(jnp.sum(p[0:3, length:].astype(F32), axis=0, keepdims=True) for p in current)
-        station_weights, energy = lax.optimization_barrier((station_weights, energy))
+        mixes = run_pick(plan, mixes)
+        station_weights, mixes, energy = lax.optimization_barrier((station_weights, mixes, energy))
         energy = summed(energy, "tm")
     else:
         current, energy = run_stage(plan, small, [source], shot=([edges_of(source)], shot_weights), name="shot_pass")
         energy = shared(energy, ("tm", "shot"))
-        station_weights = run_prepare(bundled(*station_net), station_inner_offsets, "prepare_station")
+        station_weights = run_prepare(station_net, "prepare_station")
     for i in range(ITERS):
         station = (i, energy, mixes, station_weights)
         form = {"split_in": "parts"} if paired and i == 0 else {}
@@ -664,8 +688,8 @@
             )
             edge = lax.ppermute(edge, "line", [(0, 1), (1, 0)])
             current, energy = run_stage(plan, small, [current], shot=([edge], shot_weights), name="shot_pass")
-            fresh, energy = lax.optimization_barrier((bundle, energy))
-            station_weights = run_prepare(fresh, station_inner_offsets, "prepare_station")
+            fresh, energy = lax.optimization_barrier((station_net, energy))
+            station_weights = run_prepare(fresh, "prepare_station")
             energy = shared(energy, ("tm", "shot"))
         else:
             (current,) = run_stage(plan, small, came, station=station, name="station_pass")

time: 69.7 us -> 68.3 us (0.980)
  waiting for transfers between devices: 10.3 us -> 12.2 us
  starting transfers between devices: 13.9 us -> 12.9 us
  other arithmetic: 0.94 us -> 0.1 us
  Pallas kernels: 31.6 us -> 30.8 us
    pallas_call x4, Pallas kernels: 27.4 us -> 26.2 us  [run_stage(): pl.pallas_call(functools.partial(stage_kernel, plan, station_round, shot...]
    ppermute x6, waiting for transfers between devices: 5 us -> 6.08 us  [exchanged(): lax.ppermute(parts[d], axes, [(i, i ^ d) for i in range(size)])]
    concatenate x2 -> x0, other arithmetic: 0.85 us -> none  [bundled(): return jnp.concatenate(rows, axis=0)]
    ppermute x1, starting transfers between devices: 1.55 us -> 0.79 us  [per_device(): edge = lax.ppermute(edge, 'line', [(0, 1), (1, 0)])]
    ppermute x1, waiting for transfers between devices: 2.43 us -> 3.19 us  [per_device(): edge = lax.ppermute(edge, 'line', [(0, 1), (1, 0)])]
    pad x2 -> x0, local copies, waits for them, and re-layouts: 0.7 us -> none  [bundled(): jnp.pad(entry.transpose(1, 0, 2), ((0, 0), (0, 12), (0, 0)))]
    pallas_call x1 -> x2, Pallas kernels: 1.78 us -> 2.1 us  [the longest x1 1.93 us: run_pack(): pl.pallas_call(functools.partial(pack_kernel, plan), out_shape=shapes, in...]
  transfers between devices with their start and end apart: 12 -> 12, of which waited for: 8 -> 9; matrix products, arithmetic and copies ran while one was open for 2% -> 0% of each run, Pallas kernels for 3% -> 4%
where the time goes in v1:
time: 68.3 us; the launch traced here: 68.1 us
  Pallas kernels  30.8 us (45%)
  starting transfers between devices  12.9 us (19%)
  waiting for transfers between devices  12.2 us (18%)
  blocking collectives  10.4 us (15%)
  local copies, waits for them, and re-layouts  1.62 us (2%)
    pallas_call x4, Pallas kernels, run_stage(): pl.pallas_call(functools.partial(stage_kernel, plan, station_round, shot...  26.2 us
    all_to_all x1, blocking collectives, per_device(): lax.all_to_all(current, ('tm', 'shot'), split_axis=0, concat_axis=0, tile...  10.4 us
    ppermute x6, starting transfers between devices, exchanged(): lax.ppermute(parts[d], axes, [(i, i ^ d) for i in range(size)])  7.61 us
    ppermute x6, waiting for transfers between devices, exchanged(): lax.ppermute(parts[d], axes, [(i, i ^ d) for i in range(size)])  6.08 us
    ppermute x5, starting transfers between devices, summed(): lax.ppermute(value, axis, [(i, i ^ d) for i in range(size)])  4.53 us
    ppermute x1, waiting for transfers between devices, per_device(): edge = lax.ppermute(edge, 'line', [(0, 1), (1, 0)])  3.19 us
    ppermute x5, waiting for transfers between devices, summed(): lax.ppermute(value, axis, [(i, i ^ d) for i in range(size)])  2.92 us
    pallas_call x3, Pallas kernels, run_prepare(): pl.pallas_call(prepare_kernel, out_shape=[jax.ShapeDtypeStruct((QH + 2, W...  2.44 us
  transfers between devices with their start and end apart: 12, of which 9 were waited for; matrix products, arithmetic and copies ran while one was open for 0% of the time, Pallas kernels for 4%

profile of v1, /device:TPU:0, one launch (start us, length us, event | category | flops | bytes accessed | tf_op | source)
XLA Modules:
  0.0 68.1 jit_solution(12843966101287302019)
XLA Ops:
  0.0 1.9 %pack.1 = (bf16[64,512]{1,0:T(8,128)(2,1)}, bf16[64,512]{1,0:T(8,128)(2,1)}, bf16[16,512]{1,0:T(8,128)(2,1)}, bf16[16,512]{1,0:T(8,128)(2,1)}, f32[216,64]{1,0:T(8,128)}, /*index=5*/f32[216,64]{1,0:T(8,128)}) custom-call(bf16[128,512]{1,0:T(8,128)(2,1)} %bitcast.10, bf16[3,4,64]{2,1,0:T(4,128)(2,1)} %bitcast.11, bf16[3,64,64]{2,1,0:T(8,128)(2,1)} %refs_2_.5, ...), custom_call_target="tpu_custom_call" | custom-call | flops 16777216 | bytes 1048576 | tf_op jit(solution)/shard_map/pack/pallas_call | solution.py:535
  1.9 0.5 collective-permute-start
  2.5 2.6 %collective-permute-start.1 = (bf16[16,512]{1,0:T(8,128)(2,1)}, bf16[16,512]{1,0:T(8,128)(2,1)S(1)}, u32[]{:S(2)}, u32[]{:S(2)}) collective-permute-start(bf16[16,512]{1,0:T(8,128)(2,1)} %get-tuple-element.37), channel_id=1, source_target_pairs={{0,2},{1,3},{2,0},{3,1},{4,6},{5,7},{6,4},{7,5},{8,10},{9,11},{10,... | collective-permute-start | bytes 49160 | tf_op jit(solution)/shard_map/ppermute | solution.py:569
  5.0 0.1 collective-permute-start.2
  5.1 0.9 %copy-done.2 = f32[216,64]{1,0:T(8,128)S(1)} copy-done((f32[216,64]{1,0:T(8,128)S(1)}, f32[216,64]{1,0:T(8,128)}, u32[]{:S(2)}) %copy-start.2) | copy-done | bytes 55320
  6.0 0.8 %prepare_shot.1 = (bf16[10,256,256]{2,1,0:T(8,128)(2,1)S(1)}, bf16[18,256,128]{2,1,0:T(8,128)(2,1)S(1)}) custom-call(f32[216,64]{1,0:T(8,128)S(1)} %copy-done.2), custom_call_target="tpu_custom_call" | custom-call | flops 536870912 | bytes 4194304 | tf_op jit(solution)/shard_map/prepare_shot/pallas_call | solution.py:513
  6.8 0.1 collective-permute-done.1.refs_6_
  7.0 1.4 %collective-permute-done.2.refs_7_ = bf16[16,512]{1,0:T(8,128)(2,1)S(1)} collective-permute-done((bf16[16,512]{1,0:T(8,128)(2,1)}, bf16[16,512]{1,0:T(8,128)(2,1)S(1)}, u32[]{:S(2)}, u32[]{:S(2)}) %collective-permute-start.2) | collective-permute-done | bytes 16416 | tf_op jit(solution)/shard_map/ppermute | solution.py:569
  8.5 6.6 %shot_pass.2 = (bf16[16,1152]{1,0:T(8,128)(2,1)S(1)}, bf16[16,1152]{1,0:T(8,128)(2,1)S(1)}, bf16[16,1152]{1,0:T(8,128)(2,1)S(1)}, bf16[16,1152]{1,0:T(8,128)(2,1)S(1)}) custom-call(s32[8]{0:T(128)S(1)} %copy-done.4, s32[4]{0:T(128)S(1)} %copy-done.5, s32[4]{0:T(128)S(1)} %copy-done.6, f32[2]{0:T(128)S(1)} %copy-done.7, bf16[64,512]{1,0:T(8,128)(2,1)S(1)} %copy-done.3, ...), custom_call_target="tpu_custom_call" | custom-call | flops 3758096384 | bytes 1048576 | tf_op jit(solution)/shard_map/shot_pass/pallas_call | solution.py:495
  15.1 1.6 %collective-permute-start.3 = (bf16[16,1152]{1,0:T(8,128)(2,1)S(1)}, bf16[16,1152]{1,0:T(8,128)(2,1)S(1)}, u32[]{:S(2)}, u32[]{:S(2)}) collective-permute-start(bf16[16,1152]{1,0:T(8,128)(2,1)S(1)} %get-tuple-element.44), channel_id=1, source_target_pairs={{0,4},{4,0},{8,12},{12,8},{1,5},{5,1},{9,13},{13,9},{2,6},{6,2},{1... | collective-permute-start | bytes 110600 | tf_op jit(solution)/shard_map/ppermute | solution.py:569
  16.7 2.6 %collective-permute-start.4 = (bf16[16,1152]{1,0:T(8,128)(2,1)S(1)}, bf16[16,1152]{1,0:T(8,128)(2,1)S(1)}, u32[]{:S(2)}, u32[]{:S(2)}) collective-permute-start(bf16[16,1152]{1,0:T(8,128)(2,1)S(1)} %get-tuple-element.45), channel_id=1, source_target_pairs={{0,8},{4,12},{8,0},{12,4},{1,9},{5,13},{9,1},{13,5},{2,10},{6,14},... | collective-permute-start | bytes 110600 | tf_op jit(solution)/shard_map/ppermute | solution.py:569
  19.3 0.2 collective-permute-start.5
  19.5 0.2 pick.1.refs_9_.refs_6_
  19.7 0.8 %prepare_station.2 = (bf16[10,256,256]{2,1,0:T(8,128)(2,1)S(1)}, bf16[18,256,128]{2,1,0:T(8,128)(2,1)S(1)}) custom-call(f32[216,64]{1,0:T(8,128)S(1)} %copy-done.1), custom_call_target="tpu_custom_call" | custom-call | flops 536870912 | bytes 4194304 | tf_op jit(solution)/shard_map/prepare_station/pallas_call | solution.py:513
  20.6 1.7 %collective-permute-done.4.refs_6_ = bf16[16,1152]{1,0:T(8,128)(2,1)S(1)} collective-permute-done((bf16[16,1152]{1,0:T(8,128)(2,1)S(1)}, bf16[16,1152]{1,0:T(8,128)(2,1)S(1)}, u32[]{:S(2)}, u32[]{:S(2)}) %collective-permute-start.4) | collective-permute-done | bytes 36896 | tf_op jit(solution)/shard_map/ppermute | solution.py:569
  22.3 2.7 %collective-permute-done.5.refs_7_ = bf16[16,1152]{1,0:T(8,128)(2,1)S(1)} collective-permute-done((bf16[16,1152]{1,0:T(8,128)(2,1)S(1)}, bf16[16,1152]{1,0:T(8,128)(2,1)S(1)}, u32[]{:S(2)}, u32[]{:S(2)}) %collective-permute-start.5) | collective-permute-done | bytes 36896 | tf_op jit(solution)/shard_map/ppermute | solution.py:569
  25.1 0.1 collective-permute-start.6
  25.2 1.1 %collective-permute-done.6 = f32[1,128]{1,0:T(1,128)S(1)} collective-permute-done((f32[1,128]{1,0:T(1,128)S(1)}, f32[1,128]{1,0:T(1,128)S(1)}, u32[]{:S(2)}, u32[]{:S(2)}) %collective-permute-start.6) | collective-permute-done | bytes 544 | tf_op jit(solution)/shard_map/ppermute | solution.py:643
  26.3 6.6 %station_pass.2 = (bf16[64,1024]{1,0:T(8,128)(2,1)S(1)}, bf16[16,1024]{1,0:T(8,128)(2,1)S(1)}) custom-call(s32[8]{0:T(128)S(1)} %copy-done.4, s32[4]{0:T(128)S(1)} %copy-done.5, s32[4]{0:T(128)S(1)} %copy-done.6, f32[2]{0:T(128)S(1)} %copy-done.7, bf16[16,1152]{1,0:T(8,128)(2,1)S(1)} %get-tuple-element.43.refs_4_, ...), custom_call_target="tpu_custom_call" | custom-call | flops 3758096384 | bytes 1048576 | tf_op jit(solution)/shard_map/station_pass/pallas_call | solution.py:495
  32.9 0.8 %collective-permute-start.7 = (bf16[16,1024]{1,0:T(8,128)(2,1)S(1)}, bf16[16,1024]{1,0:T(8,128)(2,1)S(1)}, u32[]{:S(2)}, u32[]{:S(2)}) collective-permute-start(bf16[16,1024]{1,0:T(8,128)(2,1)S(1)} %get-tuple-element.56), channel_id=1, source_target_pairs={{0,2},{2,0},{1,3},{3,1},{4,6},{6,4},{5,7},{7,5},{8,10},{10,8},{9,1... | collective-permute-start | bytes 98312 | tf_op jit(solution)/shard_map/ppermute | solution.py:689
  33.7 3.2 %collective-permute-done.7.refs_5_ = bf16[16,1024]{1,0:T(8,128)(2,1)S(1)} collective-permute-done((bf16[16,1024]{1,0:T(8,128)(2,1)S(1)}, bf16[16,1024]{1,0:T(8,128)(2,1)S(1)}, u32[]{:S(2)}, u32[]{:S(2)}) %collective-permute-start.7) | collective-permute-done | bytes 32800 | tf_op jit(solution)/shard_map/ppermute | solution.py:689
  36.8 6.6 %shot_pass.3 = (bf16[64,1024]{1,0:T(8,128)(2,1)S(1)}, f32[1,128]{1,0:T(1,128)S(1)}) custom-call(s32[8]{0:T(128)S(1)} %copy-done.4, s32[4]{0:T(128)S(1)} %copy-done.5, s32[4]{0:T(128)S(1)} %copy-done.6, f32[2]{0:T(128)S(1)} %copy-done.7, bf16[64,1024]{1,0:T(8,128)(2,1)S(1)} %get-tuple-element.55.refs_4_, bf16[16,1024]{1,0:T(8,128)(2,1)S(1)} %collective-permute-done.7.refs_5_, ...), custom_call_target="tpu_custom_call" | custom-call | flops 3758096384 | bytes 1048576 | tf_op jit(solution)/shard_map/shot_pass/pallas_call | solution.py:495
  43.5 0.1 collective-permute-start.8
  43.5 1.1 %collective-permute-done.8 = f32[1,128]{1,0:T(1,128)S(1)} collective-permute-done((f32[1,128]{1,0:T(1,128)S(1)}, f32[1,128]{1,0:T(1,128)S(1)}, u32[]{:S(2)}, u32[]{:S(2)}) %collective-permute-start.8) | collective-permute-done | bytes 544 | tf_op jit(solution)/shard_map/ppermute | solution.py:643
  44.6 0.5 collective-permute-start.11
  45.2 3.9 %collective-permute-start.9 = (f32[1,128]{1,0:T(1,128)S(1)}, f32[1,128]{1,0:T(1,128)S(1)}, u32[]{:S(2)}, u32[]{:S(2)}) collective-permute-start(f32[1,128]{1,0:T(1,128)S(1)} %add.58), channel_id=1, source_target_pairs={{0,4},{4,0},{8,12},{12,8},{1,5},{5,1},{9,13},{13,9},{2,6},{6,2},{1... | collective-permute-start | bytes 1544 | tf_op jit(solution)/shard_map/ppermute | solution.py:643
  49.0 0.8 %prepare_station.3 = (bf16[10,256,256]{2,1,0:T(8,128)(2,1)S(1)}, bf16[18,256,128]{2,1,0:T(8,128)(2,1)S(1)}) custom-call(f32[216,64]{1,0:T(8,128)S(1)} %copy-done.1), custom_call_target="tpu_custom_call" | custom-call | flops 536870912 | bytes 4194304 | tf_op jit(solution)/shard_map/prepare_station/pallas_call | solution.py:513
  49.8 0.1 collective-permute-done.11
  50.0 0.6 collective-permute-done.9
  50.6 6.5 %station_pass.3 = bf16[8,16,512]{2,1,0:T(8,128)(2,1)S(1)} custom-call(s32[8]{0:T(128)S(1)} %copy-done.4, s32[4]{0:T(128)S(1)} %copy-done.5, s32[4]{0:T(128)S(1)} %copy-done.6, f32[2]{0:T(128)S(1)} %copy-done.7, bf16[64,1024]{1,0:T(8,128)(2,1)S(1)} %get-tuple-element.57.refs_4_, f32[1,128]{1,0:T(1,128)S(1)} %add_add_fusion.refs_5_, ...), custom_call_target="tpu_custom_call" | custom-call | flops 3758096384 | bytes 1048576 | tf_op jit(solution)/shard_map/station_pass/pallas_call | solution.py:495
  57.0 10.4 %all_to_all.5 = bf16[8,16,512]{2,1,0:T(8,128)(2,1)S(1)} all-to-all(bf16[8,16,512]{2,1,0:T(8,128)(2,1)S(1)} %station_pass.3), channel_id=1, replica_groups=mesh['group'=2,'shot'=4,'line'=2,'tm'=2] {'tm','shot'}, dimensions={0} | all-to-all | bytes 262144 | tf_op jit(solution)/shard_map/all_to_all | solution.py:700
  67.4 0.7 %copy.15 = bf16[8,16,512]{2,1,0:T(8,128)(2,1)} copy(bf16[8,16,512]{2,0,1:T(8,128)(2,1)S(1)} %bitcast.9) | data formatting | bytes 262144 | tf_op jit(solution)/shard_map/transpose | solution.py:701
  (27 shorter events, 0.1 us)
Async XLA Ops:
  0.0 8.4 %copy-start.7 = (f32[2]{0:T(128)S(1)}, f32[2]{0:T(128)}, u32[]{:S(2)}) copy-start(f32[2]{0:T(128)} %refs_3_.9) | copy-start | bytes 28
  0.0 8.4 %copy-start.4 = (s32[8]{0:T(128)S(1)}, s32[8]{0:T(128)}, u32[]{:S(2)}) copy-start(s32[8]{0:T(128)} %refs_0_.7) | copy-start | bytes 100
  0.0 8.4 %copy-start.6 = (s32[4]{0:T(128)S(1)}, s32[4]{0:T(128)}, u32[]{:S(2)}) copy-start(s32[4]{0:T(128)} %refs_2_.9) | copy-start | bytes 52
  0.0 8.4 %copy-start.5 = (s32[4]{0:T(128)S(1)}, s32[4]{0:T(128)}, u32[]{:S(2)}) copy-start(s32[4]{0:T(128)} %refs_1_.7) | copy-start | bytes 52
  1.9 6.5 %collective-permute-start = (bf16[64,512]{1,0:T(8,128)(2,1)}, bf16[64,512]{1,0:T(8,128)(2,1)S(1)}, u32[]{:S(2)}, u32[]{:S(2)}) collective-permute-start(bf16[64,512]{1,0:T(8,128)(2,1)} %get-tuple-element.36), channel_id=1, source_target_pairs={{0,1},{1,0},{2,3},{3,2},{4,5},{5,4},{6,7},{7,6},{8,9},{9,8},{10,11... | collective-permute-start | bytes 196616 | tf_op jit(solution)/shard_map/ppermute | solution.py:569
  2.5 4.5 %collective-permute-start.1 = (bf16[16,512]{1,0:T(8,128)(2,1)}, bf16[16,512]{1,0:T(8,128)(2,1)S(1)}, u32[]{:S(2)}, u32[]{:S(2)}) collective-permute-start(bf16[16,512]{1,0:T(8,128)(2,1)} %get-tuple-element.37), channel_id=1, source_target_pairs={{0,2},{1,3},{2,0},{3,1},{4,6},{5,7},{6,4},{7,5},{8,10},{9,11},{10,... | collective-permute-start | bytes 49160 | tf_op jit(solution)/shard_map/ppermute | solution.py:569
  5.0 3.4 %collective-permute-start.2 = (bf16[16,512]{1,0:T(8,128)(2,1)}, bf16[16,512]{1,0:T(8,128)(2,1)S(1)}, u32[]{:S(2)}, u32[]{:S(2)}) collective-permute-start(bf16[16,512]{1,0:T(8,128)(2,1)} %get-tuple-element.38), channel_id=1, source_target_pairs={{0,3},{1,2},{2,1},{3,0},{4,7},{5,6},{6,5},{7,4},{8,11},{9,10},{10,... | collective-permute-start | bytes 49160 | tf_op jit(solution)/shard_map/ppermute | solution.py:569
  5.1 0.9 %copy-start.2 = (f32[216,64]{1,0:T(8,128)S(1)}, f32[216,64]{1,0:T(8,128)}, u32[]{:S(2)}) copy-start(f32[216,64]{1,0:T(8,128)} %get-tuple-element.39.bundle) | copy-start | bytes 165892
  6.0 2.4 %copy-start.3 = (bf16[64,512]{1,0:T(8,128)(2,1)S(1)}, bf16[64,512]{1,0:T(8,128)(2,1)}, u32[]{:S(2)}) copy-start(bf16[64,512]{1,0:T(8,128)(2,1)} %get-tuple-element.35.refs_4_) | copy-start | bytes 196612
  8.5 11.1 %copy-start = (bf16[2,128,1024]{2,1,0:T(8,128)(2,1)S(1)}, bf16[2,128,1024]{2,1,0:T(8,128)(2,1)}, u32[]{:S(2)}) copy-start(bf16[2,128,1024]{2,1,0:T(8,128)(2,1)} %mixes) | copy-start | bytes 1572868
  8.5 11.2 %copy-start.1 = (f32[216,64]{1,0:T(8,128)S(1)}, f32[216,64]{1,0:T(8,128)}, u32[]{:S(2)}) copy-start(f32[216,64]{1,0:T(8,128)} %get-tuple-element.60.bundle) | copy-start | bytes 165892
  15.1 5.5 %collective-permute-start.3 = (bf16[16,1152]{1,0:T(8,128)(2,1)S(1)}, bf16[16,1152]{1,0:T(8,128)(2,1)S(1)}, u32[]{:S(2)}, u32[]{:S(2)}) collective-permute-start(bf16[16,1152]{1,0:T(8,128)(2,1)S(1)} %get-tuple-element.44), channel_id=1, source_target_pairs={{0,4},{4,0},{8,12},{12,8},{1,5},{5,1},{9,13},{13,9},{2,6},{6,2},{1... | collective-permute-start | bytes 110600 | tf_op jit(solution)/shard_map/ppermute | solution.py:569
  16.7 5.6 %collective-permute-start.4 = (bf16[16,1152]{1,0:T(8,128)(2,1)S(1)}, bf16[16,1152]{1,0:T(8,128)(2,1)S(1)}, u32[]{:S(2)}, u32[]{:S(2)}) collective-permute-start(bf16[16,1152]{1,0:T(8,128)(2,1)S(1)} %get-tuple-element.45), channel_id=1, source_target_pairs={{0,8},{4,12},{8,0},{12,4},{1,9},{5,13},{9,1},{13,5},{2,10},{6,14},... | collective-permute-start | bytes 110600 | tf_op jit(solution)/shard_map/ppermute | solution.py:569
  19.3 5.8 %collective-permute-start.5 = (bf16[16,1152]{1,0:T(8,128)(2,1)S(1)}, bf16[16,1152]{1,0:T(8,128)(2,1)S(1)}, u32[]{:S(2)}, u32[]{:S(2)}) collective-permute-start(bf16[16,1152]{1,0:T(8,128)(2,1)S(1)} %get-tuple-element.46), channel_id=1, source_target_pairs={{0,12},{4,8},{8,4},{12,0},{1,13},{5,9},{9,5},{13,1},{2,14},{6,10},... | collective-permute-start | bytes 110600 | tf_op jit(solution)/shard_map/ppermute | solution.py:569
  25.1 1.2 %collective-permute-start.6 = (f32[1,128]{1,0:T(1,128)S(1)}, f32[1,128]{1,0:T(1,128)S(1)}, u32[]{:S(2)}, u32[]{:S(2)}) collective-permute-start(f32[1,128]{1,0:T(1,128)S(1)} %add_bitcast_fusion), channel_id=1, source_target_pairs={{0,1},{1,0},{2,3},{3,2},{4,5},{5,4},{6,7},{7,6},{8,9},{9,8},{10,11... | collective-permute-start | bytes 1544 | tf_op jit(solution)/shard_map/ppermute | solution.py:643
  32.9 4.0 %collective-permute-start.7 = (bf16[16,1024]{1,0:T(8,128)(2,1)S(1)}, bf16[16,1024]{1,0:T(8,128)(2,1)S(1)}, u32[]{:S(2)}, u32[]{:S(2)}) collective-permute-start(bf16[16,1024]{1,0:T(8,128)(2,1)S(1)} %get-tuple-element.56), channel_id=1, source_target_pairs={{0,2},{2,0},{1,3},{3,1},{4,6},{6,4},{5,7},{7,5},{8,10},{10,8},{9,1... | collective-permute-start | bytes 98312 | tf_op jit(solution)/shard_map/ppermute | solution.py:689
  43.5 1.2 %collective-permute-start.8 = (f32[1,128]{1,0:T(1,128)S(1)}, f32[1,128]{1,0:T(1,128)S(1)}, u32[]{:S(2)}, u32[]{:S(2)}) collective-permute-start(f32[1,128]{1,0:T(1,128)S(1)} %get-tuple-element.59), channel_id=1, source_target_pairs={{0,1},{1,0},{2,3},{3,2},{4,5},{5,4},{6,7},{7,6},{8,9},{9,8},{10,11... | collective-permute-start | bytes 1544 | tf_op jit(solution)/shard_map/ppermute | solution.py:643
  44.6 5.3 %collective-permute-start.11 = (f32[1,128]{1,0:T(1,128)S(1)}, f32[1,128]{1,0:T(1,128)S(1)}, u32[]{:S(2)}, u32[]{:S(2)}) collective-permute-start(f32[1,128]{1,0:T(1,128)S(1)} %add.58), channel_id=1, source_target_pairs={{0,12},{4,8},{8,4},{12,0},{1,13},{5,9},{9,5},{13,1},{2,14},{6,10},... | collective-permute-start | bytes 1544 | tf_op jit(solution)/shard_map/ppermute | solution.py:643
  45.2 4.8 %collective-permute-start.10 = (f32[1,128]{1,0:T(1,128)S(1)}, f32[1,128]{1,0:T(1,128)S(1)}, u32[]{:S(2)}, u32[]{:S(2)}) collective-permute-start(f32[1,128]{1,0:T(1,128)S(1)} %add.58), channel_id=1, source_target_pairs={{0,8},{4,12},{8,0},{12,4},{1,9},{5,13},{9,1},{13,5},{2,10},{6,14},... | collective-permute-start | bytes 1544 | tf_op jit(solution)/shard_map/ppermute | solution.py:643
  45.2 5.4 %collective-permute-start.9 = (f32[1,128]{1,0:T(1,128)S(1)}, f32[1,128]{1,0:T(1,128)S(1)}, u32[]{:S(2)}, u32[]{:S(2)}) collective-permute-start(f32[1,128]{1,0:T(1,128)S(1)} %add.58), channel_id=1, source_target_pairs={{0,4},{4,0},{8,12},{12,8},{1,5},{5,1},{9,13},{13,9},{2,6},{6,2},{1... | collective-permute-start | bytes 1544 | tf_op jit(solution)/shard_map/ppermute | solution.py:643

commit v2 on v1

--- a/solution.py
+++ b/solution.py
@@ -417,7 +417,7 @@
         )
     if with_shot:
         if plan.paired and not first:
-            rim[...] = edges[0][...].astype(F32)
+            rim[0 : plan.groups, :] = edges[0][...].astype(F32)
         outer = rim if plan.paired else edges[0]
         sums = shot_stage(plan, place, tallies, first, outer, shot_weights, now, scratch)
     if split_out == "parts":
@@ -443,7 +443,8 @@
         row, col = iota((16, plan.rows), 0), iota((16, plan.rows), 1)
         sent = jnp.where(place[4] == 0, plan.lines - 1, 0)
         choose = picks(col == row * plan.lines + sent)
-        results[1][...] = jnp.dot(choose, now[...].astype(BF), preferred_element_type=F32).astype(BF)
+        sent = jnp.dot(choose, now[...].astype(BF), preferred_element_type=F32)
+        results[1][...] = sent[: plan.groups].astype(BF)
 
 
 SMEM = pl.BlockSpec(memory_space=pltpu.SMEM)
@@ -475,7 +476,7 @@
     else:
         shapes = [jax.ShapeDtypeStruct((plan.rows, length), BF)]
         if split_out == "edge":
-            shapes.append(jax.ShapeDtypeStruct((16, length), BF))
+            shapes.append(jax.ShapeDtypeStruct((plan.groups, length), BF))
     if shot is not None and split_out != "parts":
         shapes.append(jax.ShapeDtypeStruct((1, SLAB), F32))
     scratch = [
@@ -566,8 +567,7 @@
 
 def exchanged(parts, axes):
     size = len(parts)
-    came = [lax.ppermute(parts[d], axes, [(i, i ^ d) for i in range(size)]) for d in range(size - 1, 0, -1)]
-    return [parts[0]] + came[::-1]
+    return [parts[0]] + [lax.ppermute(parts[d], axes, [(i, i ^ d) for i in range(size)]) for d in range(1, size)]
 
 
 def per_device(
@@ -665,11 +665,11 @@
             name="shot_pass",
         )
         station_net, mixes, own = lax.optimization_barrier((station_net, mixes, parts[0]))
-        current = exchanged([own, *parts[1:]], "shot")
+        mixes, middle = lax.optimization_barrier((run_pick(plan, mixes), parts[2:-1]))
         station_weights = run_prepare(station_net, "prepare_station")
+        station_weights, nearest = lax.optimization_barrier((station_weights, parts[1]))
+        current = exchanged([own, nearest, *middle, parts[-1]], "shot")
         energy = sum(jnp.sum(p[0:3, length:].astype(F32), axis=0, keepdims=True) for p in current)
-        mixes = run_pick(plan, mixes)
-        station_weights, mixes, energy = lax.optimization_barrier((station_weights, mixes, energy))
         energy = summed(energy, "tm")
     else:
         current, energy = run_stage(plan, small, [source], shot=([edges_of(source)], shot_weights), name="shot_pass")

time: 68.3 us -> 68 us (level)
    ppermute x6, waiting for transfers between devices: 6.08 us -> 5.14 us  [exchanged(): lax.ppermute(parts[d], axes, [(i, i ^ d) for i in range(size)])]
  transfers between devices with their start and end apart: 12 -> 12, of which waited for: 9 -> 10; matrix products, arithmetic and copies ran while one was open for 0% -> 0% of each run, Pallas kernels for 4% -> 4%
where the time goes in v2:
time: 68 us; the launch traced here: 67.8 us
  Pallas kernels  30.7 us (45%)
  starting transfers between devices  13 us (19%)
  waiting for transfers between devices  11.6 us (17%)
  blocking collectives  10.6 us (16%)
  local copies, waits for them, and re-layouts  1.62 us (2%)
    pallas_call x4, Pallas kernels, run_stage(): pl.pallas_call(functools.partial(stage_kernel, plan, station_round, shot...  26.2 us
    all_to_all x1, blocking collectives, per_device(): lax.all_to_all(current, ('tm', 'shot'), split_axis=0, concat_axis=0, tile...  10.6 us
    ppermute x6, starting transfers between devices, exchanged(): lax.ppermute(parts[d], axes, [(i, i ^ d) for i in range(size)])  7.71 us
    ppermute x6, waiting for transfers between devices, exchanged(): lax.ppermute(parts[d], axes, [(i, i ^ d) for i in range(size)])  5.14 us
    ppermute x5, starting transfers between devices, summed(): lax.ppermute(value, axis, [(i, i ^ d) for i in range(size)])  4.53 us
    ppermute x5, waiting for transfers between devices, summed(): lax.ppermute(value, axis, [(i, i ^ d) for i in range(size)])  3.42 us
    ppermute x1, waiting for transfers between devices, per_device(): edge = lax.ppermute(edge, 'line', [(0, 1), (1, 0)])  3.01 us
    pallas_call x3, Pallas kernels, run_prepare(): pl.pallas_call(prepare_kernel, out_shape=[jax.ShapeDtypeStruct((QH + 2, W...  2.42 us
  transfers between devices with their start and end apart: 12, of which 10 were waited for; matrix products, arithmetic and copies ran while one was open for 0% of the time, Pallas kernels for 4%

profile of v2, /device:TPU:0, one launch (start us, length us, event | category | flops | bytes accessed | tf_op | source)
XLA Modules:
  0.0 67.8 jit_solution(6640671830987525165)
XLA Ops:
  0.0 1.9 %pack.1 = (bf16[64,512]{1,0:T(8,128)(2,1)}, bf16[64,512]{1,0:T(8,128)(2,1)}, bf16[16,512]{1,0:T(8,128)(2,1)}, bf16[16,512]{1,0:T(8,128)(2,1)}, f32[216,64]{1,0:T(8,128)}, /*index=5*/f32[216,64]{1,0:T(8,128)}) custom-call(bf16[128,512]{1,0:T(8,128)(2,1)} %bitcast.10, bf16[3,4,64]{2,1,0:T(4,128)(2,1)} %bitcast.11, bf16[3,64,64]{2,1,0:T(8,128)(2,1)} %refs_2_.5, ...), custom_call_target="tpu_custom_call" | custom-call | flops 16777216 | bytes 1048576 | tf_op jit(solution)/shard_map/pack/pallas_call | solution.py:536
  1.9 0.5 collective-permute-start
  2.5 2.6 %collective-permute-start.1 = (bf16[16,512]{1,0:T(8,128)(2,1)}, bf16[16,512]{1,0:T(8,128)(2,1)S(1)}, u32[]{:S(2)}, u32[]{:S(2)}) collective-permute-start(bf16[16,512]{1,0:T(8,128)(2,1)} %get-tuple-element.38), channel_id=1, source_target_pairs={{0,2},{1,3},{2,0},{3,1},{4,6},{5,7},{6,4},{7,5},{8,10},{9,11},{10,... | collective-permute-start | bytes 49160 | tf_op jit(solution)/shard_map/ppermute | solution.py:570
  5.0 0.1 collective-permute-start.2
  5.1 0.9 %copy-done.2 = f32[216,64]{1,0:T(8,128)S(1)} copy-done((f32[216,64]{1,0:T(8,128)S(1)}, f32[216,64]{1,0:T(8,128)}, u32[]{:S(2)}) %copy-start.2) | copy-done | bytes 55320
  6.0 0.8 %prepare_shot.1 = (bf16[10,256,256]{2,1,0:T(8,128)(2,1)S(1)}, bf16[18,256,128]{2,1,0:T(8,128)(2,1)S(1)}) custom-call(f32[216,64]{1,0:T(8,128)S(1)} %copy-done.2), custom_call_target="tpu_custom_call" | custom-call | flops 536870912 | bytes 4194304 | tf_op jit(solution)/shard_map/prepare_shot/pallas_call | solution.py:514
  6.8 0.1 collective-permute-done.1.refs_6_
  7.0 1.4 %collective-permute-done.2.refs_7_ = bf16[16,512]{1,0:T(8,128)(2,1)S(1)} collective-permute-done((bf16[16,512]{1,0:T(8,128)(2,1)}, bf16[16,512]{1,0:T(8,128)(2,1)S(1)}, u32[]{:S(2)}, u32[]{:S(2)}) %collective-permute-start.2) | collective-permute-done | bytes 16416 | tf_op jit(solution)/shard_map/ppermute | solution.py:570
  8.5 6.6 %shot_pass.2 = (bf16[16,1152]{1,0:T(8,128)(2,1)S(1)}, bf16[16,1152]{1,0:T(8,128)(2,1)S(1)}, bf16[16,1152]{1,0:T(8,128)(2,1)S(1)}, bf16[16,1152]{1,0:T(8,128)(2,1)S(1)}) custom-call(s32[8]{0:T(128)S(1)} %copy-done.4, s32[4]{0:T(128)S(1)} %copy-done.5, s32[4]{0:T(128)S(1)} %copy-done.6, f32[2]{0:T(128)S(1)} %copy-done.7, bf16[64,512]{1,0:T(8,128)(2,1)S(1)} %copy-done.3, ...), custom_call_target="tpu_custom_call" | custom-call | flops 3758096384 | bytes 1048576 | tf_op jit(solution)/shard_map/shot_pass/pallas_call | solution.py:496
  15.1 3.7 %collective-permute-start.5 = (bf16[16,1152]{1,0:T(8,128)(2,1)S(1)}, bf16[16,1152]{1,0:T(8,128)(2,1)S(1)}, u32[]{:S(2)}, u32[]{:S(2)}) collective-permute-start(bf16[16,1152]{1,0:T(8,128)(2,1)S(1)} %get-tuple-element.53), channel_id=1, source_target_pairs={{0,12},{4,8},{8,4},{12,0},{1,13},{5,9},{9,5},{13,1},{2,14},{6,10},... | collective-permute-start | bytes 110600 | tf_op jit(solution)/shard_map/ppermute | solution.py:570
  18.7 0.2 pick.1.refs_9_.refs_6_
  19.0 0.8 %prepare_station.2 = (bf16[10,256,256]{2,1,0:T(8,128)(2,1)S(1)}, bf16[18,256,128]{2,1,0:T(8,128)(2,1)S(1)}) custom-call(f32[216,64]{1,0:T(8,128)S(1)} %copy-done.1), custom_call_target="tpu_custom_call" | custom-call | flops 536870912 | bytes 4194304 | tf_op jit(solution)/shard_map/prepare_station/pallas_call | solution.py:514
  19.8 0.8 %collective-permute-start.3 = (bf16[16,1152]{1,0:T(8,128)(2,1)S(1)}, bf16[16,1152]{1,0:T(8,128)(2,1)S(1)}, u32[]{:S(2)}, u32[]{:S(2)}) collective-permute-start(bf16[16,1152]{1,0:T(8,128)(2,1)S(1)} %get-tuple-element.49), channel_id=1, source_target_pairs={{0,4},{4,0},{8,12},{12,8},{1,5},{5,1},{9,13},{13,9},{2,6},{6,2},{1... | collective-permute-start | bytes 110600 | tf_op jit(solution)/shard_map/ppermute | solution.py:570
  20.6 0.3 collective-permute-done.5.refs_7_
  20.9 2.9 %collective-permute-done.4.refs_6_ = bf16[16,1152]{1,0:T(8,128)(2,1)S(1)} collective-permute-done((bf16[16,1152]{1,0:T(8,128)(2,1)S(1)}, bf16[16,1152]{1,0:T(8,128)(2,1)S(1)}, u32[]{:S(2)}, u32[]{:S(2)}) %collective-permute-start.4) | collective-permute-done | bytes 36896 | tf_op jit(solution)/shard_map/ppermute | solution.py:570
  23.9 0.3 collective-permute-done.3.refs_5_
  24.3 1.1 %collective-permute-done.6 = f32[1,128]{1,0:T(1,128)S(1)} collective-permute-done((f32[1,128]{1,0:T(1,128)S(1)}, f32[1,128]{1,0:T(1,128)S(1)}, u32[]{:S(2)}, u32[]{:S(2)}) %collective-permute-start.6) | collective-permute-done | bytes 544 | tf_op jit(solution)/shard_map/ppermute | solution.py:643
  25.4 6.6 %station_pass.2 = (bf16[64,1024]{1,0:T(8,128)(2,1)S(1)}, bf16[8,1024]{1,0:T(8,128)(2,1)S(1)}) custom-call(s32[8]{0:T(128)S(1)} %copy-done.4, s32[4]{0:T(128)S(1)} %copy-done.5, s32[4]{0:T(128)S(1)} %copy-done.6, f32[2]{0:T(128)S(1)} %copy-done.7, bf16[16,1152]{1,0:T(8,128)(2,1)S(1)} %get-tuple-element.44.refs_4_, ...), custom_call_target="tpu_custom_call" | custom-call | flops 3758096384 | bytes 1048576 | tf_op jit(solution)/shard_map/station_pass/pallas_call | solution.py:496
  32.0 0.8 %collective-permute-start.7 = (bf16[8,1024]{1,0:T(8,128)(2,1)S(1)}, bf16[8,1024]{1,0:T(8,128)(2,1)S(1)}, u32[]{:S(2)}, u32[]{:S(2)}) collective-permute-start(bf16[8,1024]{1,0:T(8,128)(2,1)S(1)} %get-tuple-element.58), channel_id=1, source_target_pairs={{0,2},{2,0},{1,3},{3,1},{4,6},{6,4},{5,7},{7,5},{8,10},{10,8},{9,1... | collective-permute-start | bytes 49160 | tf_op jit(solution)/shard_map/ppermute | solution.py:689
  32.8 3.0 %collective-permute-done.7.refs_5_ = bf16[8,1024]{1,0:T(8,128)(2,1)S(1)} collective-permute-done((bf16[8,1024]{1,0:T(8,128)(2,1)S(1)}, bf16[8,1024]{1,0:T(8,128)(2,1)S(1)}, u32[]{:S(2)}, u32[]{:S(2)}) %collective-permute-start.7) | collective-permute-done | bytes 16416 | tf_op jit(solution)/shard_map/ppermute | solution.py:689
  35.8 6.6 %shot_pass.3 = (bf16[64,1024]{1,0:T(8,128)(2,1)S(1)}, f32[1,128]{1,0:T(1,128)S(1)}) custom-call(s32[8]{0:T(128)S(1)} %copy-done.4, s32[4]{0:T(128)S(1)} %copy-done.5, s32[4]{0:T(128)S(1)} %copy-done.6, f32[2]{0:T(128)S(1)} %copy-done.7, bf16[64,1024]{1,0:T(8,128)(2,1)S(1)} %get-tuple-element.57.refs_4_, bf16[8,1024]{1,0:T(8,128)(2,1)S(1)} %collective-permute-done.7.refs_5_, ...), custom_call_target="tpu_custom_call" | custom-call | flops 3758096384 | bytes 1048576 | tf_op jit(solution)/shard_map/shot_pass/pallas_call | solution.py:496
  42.4 0.1 collective-permute-start.8
  42.5 1.1 %collective-permute-done.8 = f32[1,128]{1,0:T(1,128)S(1)} collective-permute-done((f32[1,128]{1,0:T(1,128)S(1)}, f32[1,128]{1,0:T(1,128)S(1)}, u32[]{:S(2)}, u32[]{:S(2)}) %collective-permute-start.8) | collective-permute-done | bytes 544 | tf_op jit(solution)/shard_map/ppermute | solution.py:643
  43.6 2.0 %collective-permute-start.11 = (f32[1,128]{1,0:T(1,128)S(1)}, f32[1,128]{1,0:T(1,128)S(1)}, u32[]{:S(2)}, u32[]{:S(2)}) collective-permute-start(f32[1,128]{1,0:T(1,128)S(1)} %add.58), channel_id=1, source_target_pairs={{0,12},{4,8},{8,4},{12,0},{1,13},{5,9},{9,5},{13,1},{2,14},{6,10},... | collective-permute-start | bytes 1544 | tf_op jit(solution)/shard_map/ppermute | solution.py:643
  45.6 0.5 collective-permute-start.10
  46.1 1.9 %collective-permute-start.9 = (f32[1,128]{1,0:T(1,128)S(1)}, f32[1,128]{1,0:T(1,128)S(1)}, u32[]{:S(2)}, u32[]{:S(2)}) collective-permute-start(f32[1,128]{1,0:T(1,128)S(1)} %add.58), channel_id=1, source_target_pairs={{0,4},{4,0},{8,12},{12,8},{1,5},{5,1},{9,13},{13,9},{2,6},{6,2},{1... | collective-permute-start | bytes 1544 | tf_op jit(solution)/shard_map/ppermute | solution.py:643
  48.0 0.8 %prepare_station.3 = (bf16[10,256,256]{2,1,0:T(8,128)(2,1)S(1)}, bf16[18,256,128]{2,1,0:T(8,128)(2,1)S(1)}) custom-call(f32[216,64]{1,0:T(8,128)S(1)} %copy-done.1), custom_call_target="tpu_custom_call" | custom-call | flops 536870912 | bytes 4194304 | tf_op jit(solution)/shard_map/prepare_station/pallas_call | solution.py:514
  48.8 0.1 collective-permute-done.11
  48.9 1.1 %collective-permute-done.10 = f32[1,128]{1,0:T(1,128)S(1)} collective-permute-done((f32[1,128]{1,0:T(1,128)S(1)}, f32[1,128]{1,0:T(1,128)S(1)}, u32[]{:S(2)}, u32[]{:S(2)}) %collective-permute-start.10) | collective-permute-done | bytes 544 | tf_op jit(solution)/shard_map/ppermute | solution.py:643
  50.0 6.5 %station_pass.3 = bf16[8,16,512]{2,1,0:T(8,128)(2,1)S(1)} custom-call(s32[8]{0:T(128)S(1)} %copy-done.4, s32[4]{0:T(128)S(1)} %copy-done.5, s32[4]{0:T(128)S(1)} %copy-done.6, f32[2]{0:T(128)S(1)} %copy-done.7, bf16[64,1024]{1,0:T(8,128)(2,1)S(1)} %get-tuple-element.59.refs_4_, f32[1,128]{1,0:T(1,128)S(1)} %add_add_fusion.refs_5_, ...), custom_call_target="tpu_custom_call" | custom-call | flops 3758096384 | bytes 1048576 | tf_op jit(solution)/shard_map/station_pass/pallas_call | solution.py:496
  56.5 10.6 %all_to_all.5 = bf16[8,16,512]{2,1,0:T(8,128)(2,1)S(1)} all-to-all(bf16[8,16,512]{2,1,0:T(8,128)(2,1)S(1)} %station_pass.3), channel_id=1, replica_groups=mesh['group'=2,'shot'=4,'line'=2,'tm'=2] {'tm','shot'}, dimensions={0} | all-to-all | bytes 262144 | tf_op jit(solution)/shard_map/all_to_all | solution.py:700
  67.1 0.7 %copy.15 = bf16[8,16,512]{2,1,0:T(8,128)(2,1)} copy(bf16[8,16,512]{2,0,1:T(8,128)(2,1)S(1)} %bitcast.9) | data formatting | bytes 262144 | tf_op jit(solution)/shard_map/transpose | solution.py:701
  (27 shorter events, 0.3 us)
Async XLA Ops:
  0.0 8.4 %copy-start.7 = (f32[2]{0:T(128)S(1)}, f32[2]{0:T(128)}, u32[]{:S(2)}) copy-start(f32[2]{0:T(128)} %refs_3_.9) | copy-start | bytes 28
  0.0 8.4 %copy-start.4 = (s32[8]{0:T(128)S(1)}, s32[8]{0:T(128)}, u32[]{:S(2)}) copy-start(s32[8]{0:T(128)} %refs_0_.7) | copy-start | bytes 100
  0.0 8.4 %copy-start.6 = (s32[4]{0:T(128)S(1)}, s32[4]{0:T(128)}, u32[]{:S(2)}) copy-start(s32[4]{0:T(128)} %refs_2_.9) | copy-start | bytes 52
  0.0 8.4 %copy-start.5 = (s32[4]{0:T(128)S(1)}, s32[4]{0:T(128)}, u32[]{:S(2)}) copy-start(s32[4]{0:T(128)} %refs_1_.7) | copy-start | bytes 52
  1.9 6.5 %collective-permute-start = (bf16[64,512]{1,0:T(8,128)(2,1)}, bf16[64,512]{1,0:T(8,128)(2,1)S(1)}, u32[]{:S(2)}, u32[]{:S(2)}) collective-permute-start(bf16[64,512]{1,0:T(8,128)(2,1)} %get-tuple-element.37), channel_id=1, source_target_pairs={{0,1},{1,0},{2,3},{3,2},{4,5},{5,4},{6,7},{7,6},{8,9},{9,8},{10,11... | collective-permute-start | bytes 196616 | tf_op jit(solution)/shard_map/ppermute | solution.py:570
  2.5 4.5 %collective-permute-start.1 = (bf16[16,512]{1,0:T(8,128)(2,1)}, bf16[16,512]{1,0:T(8,128)(2,1)S(1)}, u32[]{:S(2)}, u32[]{:S(2)}) collective-permute-start(bf16[16,512]{1,0:T(8,128)(2,1)} %get-tuple-element.38), channel_id=1, source_target_pairs={{0,2},{1,3},{2,0},{3,1},{4,6},{5,7},{6,4},{7,5},{8,10},{9,11},{10,... | collective-permute-start | bytes 49160 | tf_op jit(solution)/shard_map/ppermute | solution.py:570
  5.0 3.4 %collective-permute-start.2 = (bf16[16,512]{1,0:T(8,128)(2,1)}, bf16[16,512]{1,0:T(8,128)(2,1)S(1)}, u32[]{:S(2)}, u32[]{:S(2)}) collective-permute-start(bf16[16,512]{1,0:T(8,128)(2,1)} %get-tuple-element.39), channel_id=1, source_target_pairs={{0,3},{1,2},{2,1},{3,0},{4,7},{5,6},{6,5},{7,4},{8,11},{9,10},{10,... | collective-permute-start | bytes 49160 | tf_op jit(solution)/shard_map/ppermute | solution.py:570
  5.1 0.9 %copy-start.2 = (f32[216,64]{1,0:T(8,128)S(1)}, f32[216,64]{1,0:T(8,128)}, u32[]{:S(2)}) copy-start(f32[216,64]{1,0:T(8,128)} %get-tuple-element.40.bundle) | copy-start | bytes 165892
  6.0 2.4 %copy-start.3 = (bf16[64,512]{1,0:T(8,128)(2,1)S(1)}, bf16[64,512]{1,0:T(8,128)(2,1)}, u32[]{:S(2)}) copy-start(bf16[64,512]{1,0:T(8,128)(2,1)} %get-tuple-element.36.refs_4_) | copy-start | bytes 196612
  8.5 10.3 %copy-start = (bf16[2,128,1024]{2,1,0:T(8,128)(2,1)S(1)}, bf16[2,128,1024]{2,1,0:T(8,128)(2,1)}, u32[]{:S(2)}) copy-start(bf16[2,128,1024]{2,1,0:T(8,128)(2,1)} %mixes) | copy-start | bytes 1572868
  8.5 10.5 %copy-start.1 = (f32[216,64]{1,0:T(8,128)S(1)}, f32[216,64]{1,0:T(8,128)}, u32[]{:S(2)}) copy-start(f32[216,64]{1,0:T(8,128)} %get-tuple-element.62.bundle) | copy-start | bytes 165892
  15.1 5.8 %collective-permute-start.5 = (bf16[16,1152]{1,0:T(8,128)(2,1)S(1)}, bf16[16,1152]{1,0:T(8,128)(2,1)S(1)}, u32[]{:S(2)}, u32[]{:S(2)}) collective-permute-start(bf16[16,1152]{1,0:T(8,128)(2,1)S(1)} %get-tuple-element.53), channel_id=1, source_target_pairs={{0,12},{4,8},{8,4},{12,0},{1,13},{5,9},{9,5},{13,1},{2,14},{6,10},... | collective-permute-start | bytes 110600 | tf_op jit(solution)/shard_map/ppermute | solution.py:570
  18.9 4.9 %collective-permute-start.4 = (bf16[16,1152]{1,0:T(8,128)(2,1)S(1)}, bf16[16,1152]{1,0:T(8,128)(2,1)S(1)}, u32[]{:S(2)}, u32[]{:S(2)}) collective-permute-start(bf16[16,1152]{1,0:T(8,128)(2,1)S(1)} %get-tuple-element.52), channel_id=1, source_target_pairs={{0,8},{4,12},{8,0},{12,4},{1,9},{5,13},{9,1},{13,5},{2,10},{6,14},... | collective-permute-start | bytes 110600 | tf_op jit(solution)/shard_map/ppermute | solution.py:570
  19.8 4.4 %collective-permute-start.3 = (bf16[16,1152]{1,0:T(8,128)(2,1)S(1)}, bf16[16,1152]{1,0:T(8,128)(2,1)S(1)}, u32[]{:S(2)}, u32[]{:S(2)}) collective-permute-start(bf16[16,1152]{1,0:T(8,128)(2,1)S(1)} %get-tuple-element.49), channel_id=1, source_target_pairs={{0,4},{4,0},{8,12},{12,8},{1,5},{5,1},{9,13},{13,9},{2,6},{6,2},{1... | collective-permute-start | bytes 110600 | tf_op jit(solution)/shard_map/ppermute | solution.py:570
  24.2 1.2 %collective-permute-start.6 = (f32[1,128]{1,0:T(1,128)S(1)}, f32[1,128]{1,0:T(1,128)S(1)}, u32[]{:S(2)}, u32[]{:S(2)}) collective-permute-start(f32[1,128]{1,0:T(1,128)S(1)} %add_bitcast_fusion), channel_id=1, source_target_pairs={{0,1},{1,0},{2,3},{3,2},{4,5},{5,4},{6,7},{7,6},{8,9},{9,8},{10,11... | collective-permute-start | bytes 1544 | tf_op jit(solution)/shard_map/ppermute | solution.py:643
  32.0 3.8 %collective-permute-start.7 = (bf16[8,1024]{1,0:T(8,128)(2,1)S(1)}, bf16[8,1024]{1,0:T(8,128)(2,1)S(1)}, u32[]{:S(2)}, u32[]{:S(2)}) collective-permute-start(bf16[8,1024]{1,0:T(8,128)(2,1)S(1)} %get-tuple-element.58), channel_id=1, source_target_pairs={{0,2},{2,0},{1,3},{3,1},{4,6},{6,4},{5,7},{7,5},{8,10},{10,8},{9,1... | collective-permute-start | bytes 49160 | tf_op jit(solution)/shard_map/ppermute | solution.py:689
  42.4 1.2 %collective-permute-start.8 = (f32[1,128]{1,0:T(1,128)S(1)}, f32[1,128]{1,0:T(1,128)S(1)}, u32[]{:S(2)}, u32[]{:S(2)}) collective-permute-start(f32[1,128]{1,0:T(1,128)S(1)} %get-tuple-element.61), channel_id=1, source_target_pairs={{0,1},{1,0},{2,3},{3,2},{4,5},{5,4},{6,7},{7,6},{8,9},{9,8},{10,11... | collective-permute-start | bytes 1544 | tf_op jit(solution)/shard_map/ppermute | solution.py:643
  43.6 5.3 %collective-permute-start.11 = (f32[1,128]{1,0:T(1,128)S(1)}, f32[1,128]{1,0:T(1,128)S(1)}, u32[]{:S(2)}, u32[]{:S(2)}) collective-permute-start(f32[1,128]{1,0:T(1,128)S(1)} %add.58), channel_id=1, source_target_pairs={{0,12},{4,8},{8,4},{12,0},{1,13},{5,9},{9,5},{13,1},{2,14},{6,10},... | collective-permute-start | bytes 1544 | tf_op jit(solution)/shard_map/ppermute | solution.py:643
  45.6 4.4 %collective-permute-start.10 = (f32[1,128]{1,0:T(1,128)S(1)}, f32[1,128]{1,0:T(1,128)S(1)}, u32[]{:S(2)}, u32[]{:S(2)}) collective-permute-start(f32[1,128]{1,0:T(1,128)S(1)} %add.58), channel_id=1, source_target_pairs={{0,8},{4,12},{8,0},{12,4},{1,9},{5,13},{9,1},{13,5},{2,10},{6,14},... | collective-permute-start | bytes 1544 | tf_op jit(solution)/shard_map/ppermute | solution.py:643
  46.1 3.9 %collective-permute-start.9 = (f32[1,128]{1,0:T(1,128)S(1)}, f32[1,128]{1,0:T(1,128)S(1)}, u32[]{:S(2)}, u32[]{:S(2)}) collective-permute-start(f32[1,128]{1,0:T(1,128)S(1)} %add.58), channel_id=1, source_target_pairs={{0,4},{4,0},{8,12},{12,8},{1,5},{5,1},{9,13},{13,9},{2,6},{6,2},{1... | collective-permute-start | bytes 1544 | tf_op jit(solution)/shard_map/ppermute | solution.py:643
